TPU v7x, 512 devices: a whole 4x8x8 slice. The times are simulated.
512 devices in a mesh: ctx: 128 (over x, z, y_hi, core), ch: 4 (over y_lo).
Axes of the slice: x: 4, y: 8 (y_hi: 2, y_lo: 4; y = y_hi * 4 + y_lo), z: 8, core: 2. Of those that a mesh axis runs over, the one named last changes fastest.
Arguments:
- hyena_q: bfloat16 [16384, 4096], P('ctx', 'ch'), may hold values from -6 to 6
- hyena_k: bfloat16 [16384, 4096], P('ctx', 'ch'), may hold values from -6 to 6
- hyena_v: bfloat16 [16384, 4096], P('ctx', 'ch'), may hold values from -6 to 6
- short_taps: float32 [3, 3, 4096], P(None, None, 'ch'), may hold values from -3 to 3
- residues: float32 [16, 4096], P(None, 'ch'), may hold values from -1.5 to 1.5
- rates: float32 [16, 4096], P(None, 'ch'), may hold values from 6.1035157e-06 to 0.05
- queries: bfloat16 [16384, 4096], P('ctx', 'ch'), may hold values from -6 to 6
- keys: bfloat16 [16384, 4096], P('ctx', 'ch'), may hold values from -6 to 6
- offsets: int32 [128], replicated, may hold values from 0 to 24384, as said below
- block_mask: int32 [128, 6], P('ctx'), may hold values from 0 to 1, as said below
- out_gain: float32 [4096], P('ch'), may hold values from 0.5 to 1.5
Outputs:
- hyena_out: bfloat16 [16384, 4096], P('ctx', 'ch')
- attn_out: bfloat16 [16384, 4096], P('ctx', 'ch')
Inputs may be any that keep to these rules, and one draw needn't show every extreme that they name: offsets[0] is 0, each offset exceeds the one before by 128 to 256, and the last offset is exactly (128 - 1) * 192. `block_mask`: columns 0 and 1 are 1 in every row.
All inputs are finite; a program needn't handle non-finite values.
Results may differ from a plain program's by a relative error of at most 0.029.
Values may be sent and summed in bfloat16 or wider, within the bound.
No kernel may reach another device: no remote copies, remote signals or barrier semaphores. Data moves between devices by JAX's collectives and lax.ppermute only.
A program may use at most 128 MiB of HBM per device.

v0:
```python
from functools import partial
import math

import jax
import jax.numpy as jnp
from jax import lax
from jax.sharding import PartitionSpec as P

HEAD_DIM = 128
SUB = 32
STEPS = 6


orig_window = 8192.0
rope_base = 10000.0
yarn_factor = 128.0
norm_eps = 1e-05
highest = lax.Precision.HIGHEST


def passed_along(value, axis, steps):
    count = lax.axis_size(axis)
    first, last = (max(0, -steps), min(count, count - steps))
    return lax.ppermute(value, axis, [(source, source + steps) for source in range(first, last)])


def shifted(block, axis, distance):
    devices = range(lax.axis_size(axis))
    route = [((i - distance) % len(devices), i) for i in devices]
    return lax.ppermute(block, axis, route)


def head_freqs(head_dim):
    half_dim = head_dim // 2
    base_freq = jnp.power(rope_base, -2.0 * jnp.arange(half_dim, dtype=jnp.float32) / head_dim)
    wave_ratio = orig_window * base_freq / (2.0 * math.pi)
    ramp_mix = jnp.clip((wave_ratio - 1.0) / 31.0, 0.0, 1.0)
    freq_table = base_freq * ramp_mix + base_freq / yarn_factor * (1.0 - ramp_mix)
    yarn_scale = 0.1 * math.log(yarn_factor) + 1.0
    return (freq_table, yarn_scale)


def rotate(x, positions, freq_table):
    half_dim = x.shape[2] // 2
    angles = positions.astype(jnp.float32)[:, None, None] * freq_table[None, None, :]
    cosine = jnp.cos(angles)
    sine = jnp.sin(angles)
    lead_half = x[:, :, :half_dim]
    tail_half = x[:, :, half_dim:]
    return jnp.concatenate(
        [lead_half * cosine - tail_half * sine, tail_half * cosine + lead_half * sine], axis=2
    )


def featurize(x, before, tap_set):
    extended = jnp.concatenate([before.astype(jnp.float32), x.astype(jnp.float32)], axis=0)
    count = x.shape[0]
    return (
        tap_set[0] * extended[2:]
        + tap_set[1] * extended[1 : count + 1]
        + tap_set[2] * extended[:count]
    )


def modal_tables(residues, rates, sub):
    gain_mode = residues * jnp.sqrt(-jnp.expm1(-2.0 * rates))
    step_idx = jnp.arange(sub, dtype=jnp.int32)
    lag_value = step_idx.astype(jnp.float32)
    filter_sub = jnp.einsum(
        "mc,mnc->nc",
        gain_mode,
        jnp.exp(-rates[:, None, :] * lag_value[None, :, None]),
        precision=highest,
    )
    lag_index = step_idx[:, None] - step_idx[None, :]
    one_hot = (lag_index[:, :, None] == step_idx[None, None, :]).astype(jnp.float32)
    toeplitz = jnp.einsum("tsn,nc->tsc", one_hot, filter_sub, precision=highest)
    end_decay = jnp.exp(-rates[:, None, :] * (sub - 1.0 - lag_value)[None, :, None])
    read_decay = gain_mode[:, None, :] * jnp.exp(
        -rates[:, None, :] * (lag_value + 1.0)[None, :, None]
    )
    return (toeplitz, end_decay, read_decay)


def stretch_local(mixed, toeplitz, end_decay, rates, sub):
    tok_rows, chan_count = mixed.shape
    sub_count = tok_rows // sub
    blocks = mixed.reshape(sub_count, sub, chan_count)
    near_part = jnp.einsum("tsc,bsc->btc", toeplitz, blocks, precision=highest).reshape(
        tok_rows, chan_count
    )
    inflow = jnp.einsum("msc,bsc->bmc", end_decay, blocks, precision=highest)
    step_decay = jnp.exp(-rates * sub)

    def advance(state_now, block_in):
        return (step_decay * state_now + block_in, state_now)

    final_state, start_state = lax.scan(advance, jnp.zeros_like(rates), inflow)
    return (near_part, start_state, final_state)


def stretch_far(read_decay, start_state, carry_in, rates, sub):
    sub_count = start_state.shape[0]
    lead_span = (sub * jnp.arange(sub_count, dtype=jnp.int32)).astype(jnp.float32)
    lead_decay = jnp.exp(-rates[None, :, :] * lead_span[:, None, None])
    full_state = start_state + lead_decay * carry_in[None, :, :]
    far_part = jnp.einsum("mtc,bmc->btc", read_decay, full_state, precision=highest)
    return far_part.reshape(sub_count * sub, rates.shape[1])


def absorb(carry_all, q_rot, score_coef, key_block, value_block, visible):
    run_max, run_sum, run_acc = carry_all
    scores = (
        jnp.einsum("qhd,khd->hqk", q_rot, key_block, preferred_element_type=jnp.float32)
        * score_coef
    )
    masked = jnp.where(visible[None], scores, -1e30)
    new_max = jnp.maximum(run_max, jnp.max(masked, axis=2))
    rescale = jnp.exp(run_max - new_max)
    weights = jnp.where(visible[None], jnp.exp(masked - new_max[:, :, None]), 0.0)
    run_sum = run_sum * rescale + jnp.sum(weights, axis=2)
    update = jnp.einsum(
        "hqk,khd->qhd",
        weights.astype(jnp.bfloat16),
        value_block,
        preferred_element_type=jnp.float32,
    )
    run_acc = run_acc * jnp.transpose(rescale)[:, :, None] + update
    return (new_max, run_sum, run_acc)


def local(
    hyena_q,
    hyena_k,
    hyena_v,
    short_taps,
    residues,
    rates,
    queries,
    keys,
    offsets,
    block_mask,
    out_gain,
):
    tok_rows, feat_width = queries.shape
    head_count = feat_width // HEAD_DIM
    ctx_count = lax.axis_size("ctx")
    my_index = lax.axis_index("ctx")
    rim_rows = jnp.stack(
        [hyena_q[tok_rows - 2 :], hyena_k[tok_rows - 2 :], hyena_v[tok_rows - 2 :]]
    )
    halo_rows = passed_along(rim_rows, "ctx", 1)
    feat_q = featurize(hyena_q, halo_rows[0], short_taps[0])
    feat_k = featurize(hyena_k, halo_rows[1], short_taps[1])
    feat_v = featurize(hyena_v, halo_rows[2], short_taps[2])
    mixed = feat_k * feat_v
    toeplitz, end_decay, read_decay = modal_tables(residues, rates, SUB)
    near_part, start_state, final_state = stretch_local(mixed, toeplitz, end_decay, rates, SUB)
    stretch_decay = jnp.exp(-rates * tok_rows)

    def relay_state(turn_index, carry_in):
        return passed_along(
            (stretch_decay * carry_in + final_state).astype(jnp.bfloat16), "ctx", 1
        ).astype(jnp.float32)

    carry_in = lax.fori_loop(0, ctx_count - 1, relay_state, jnp.zeros_like(final_state))
    far_part = stretch_far(read_decay, start_state, carry_in, rates, SUB)
    hyena_out = (feat_q * (near_part + far_part)).astype(jnp.bfloat16)
    freq_table, yarn_scale = head_freqs(HEAD_DIM)
    score_coef = yarn_scale * yarn_scale / math.sqrt(HEAD_DIM)
    position = jnp.arange(tok_rows, dtype=jnp.int32)
    query_pos = offsets[my_index] + position
    q_rot = rotate(
        queries.reshape(tok_rows, head_count, HEAD_DIM).astype(jnp.float32), query_pos, freq_table
    ).astype(jnp.bfloat16)
    k_rot = rotate(
        keys.reshape(tok_rows, head_count, HEAD_DIM).astype(jnp.float32), query_pos, freq_table
    ).astype(jnp.bfloat16)
    v_own = hyena_out.reshape(tok_rows, head_count, HEAD_DIM)
    carry_all = (
        jnp.full((head_count, tok_rows), -1e30, jnp.float32),
        jnp.zeros((head_count, tok_rows), jnp.float32),
        jnp.zeros((tok_rows, head_count, HEAD_DIM), jnp.float32),
    )
    kv_block = (k_rot, v_own)
    for step_back in range(STEPS):
        if step_back > 0:
            kv_block = shifted((kv_block[0], kv_block[1]), "ctx", 1)
        key_block, value_block = kv_block
        allowed = block_mask[0, step_back] == 1
        if step_back == 0:
            visible = (position[None, :] <= position[:, None]) & allowed
        else:
            visible = jnp.broadcast_to(allowed, (tok_rows, tok_rows))
        step_fn = partial(
            absorb,
            q_rot=q_rot,
            score_coef=score_coef,
            key_block=key_block,
            value_block=value_block,
            visible=visible,
        )
        carry_all = step_fn(carry_all)
    run_max, run_sum, run_acc = carry_all
    attended = (run_acc / jnp.transpose(run_sum)[:, :, None]).reshape(tok_rows, feat_width)
    squares = jnp.sum(attended * attended, axis=1)
    sq_total = lax.psum(squares, "ch")
    feat_total = feat_width * lax.axis_size("ch")
    attn_out = (
        attended * lax.rsqrt(sq_total / feat_total + norm_eps)[:, None] * out_gain[None, :]
    ).astype(jnp.bfloat16)
    return (hyena_out, attn_out)


def solution(mesh):
    return jax.shard_map(
        local,
        mesh=mesh,
        in_specs=(
            P("ctx", "ch"),
            P("ctx", "ch"),
            P("ctx", "ch"),
            P(None, None, "ch"),
            P(None, "ch"),
            P(None, "ch"),
            P("ctx", "ch"),
            P("ctx", "ch"),
            P(),
            P("ctx", None),
            P("ch"),
        ),
        out_specs=(P("ctx", "ch"), P("ctx", "ch")),
        check_vma=False,
    )
```

profile of v0, /device:TPU:6, one launch (start us, length us, event | category | flops | bytes accessed | tf_op | source)
XLA Modules:
  0.0 1757.2 jit_solution(1747015296036417766)
XLA Ops:
  34.0 14.3 copy.51
  49.5 29.6 %fusion.131 = f32[1024,4,32]{2,1,0:T(4,128)} fusion(f32[4,32,1024]{1,0,2:T(4,128)S(1)} %copy.29, f32[32,32,1024]{1,0,2:T(8,128)} %copy.51), kind=kOutput, calls=%fused_computation.198 | convolution fusion | flops 50331648 | bytes 5242880 | tf_op jit(solution)/shard_map/tsc,bsc->btc/dot_general | solution.py:89
  79.1 14.9 fusion.19
  98.7 1546.2 %while.25 = (s32[]{:T(128)}, f32[16,1024]{1,0:T(8,128)S(1)}, f32[16,1024]{1,0:T(8,128)S(1)}, f32[16,1024]{1,0:T(8,128)S(1)}, s32[]{:T(128)}, /*index=5*/s32[]{:T(128)}) while((s32[]{:T(128)}, f32[16,1024]{1,0:T(8,128)S(1)}, f32[16,1024]{1,0:T(8,128)S(1)}, f32[16,1024]{1,0:T(8,128)S(1)}, s32[]{:T(128)}, /*index=5*/s32[]{:T(128)}) %tuple.95), condition=%wide.region_3.4_spmd.clone, body=%wide.region_2.3_spmd.clone.sunk | while | flops 81923 | bytes 458871 | solution.py:166
  112.9 10.2 collective-permute-done
  125.0 10.2 collective-permute-done
  137.2 10.2 collective-permute-done
  149.4 10.2 collective-permute-done
  198.1 10.2 collective-permute-done
  210.3 10.2 collective-permute-done
  222.4 10.2 collective-permute-done
  234.6 10.2 collective-permute-done
  271.1 10.2 collective-permute-done
  283.3 10.2 collective-permute-done
  295.5 10.2 collective-permute-done
  307.7 10.2 collective-permute-done
  344.2 10.2 collective-permute-done
  356.4 10.2 collective-permute-done
  368.5 10.2 collective-permute-done
  380.7 10.2 collective-permute-done
  429.4 10.2 collective-permute-done
  441.6 10.2 collective-permute-done
  453.8 10.2 collective-permute-done
  465.9 10.2 collective-permute-done
  502.5 10.2 collective-permute-done
  514.6 10.2 collective-permute-done
  526.8 10.2 collective-permute-done
  539.0 10.2 collective-permute-done
  575.5 10.2 collective-permute-done
  587.7 10.2 collective-permute-done
  599.9 10.2 collective-permute-done
  612.0 10.2 collective-permute-done
  660.7 10.2 collective-permute-done
  672.9 10.2 collective-permute-done
  685.1 10.2 collective-permute-done
  697.3 10.2 collective-permute-done
  733.8 10.2 collective-permute-done
  746.0 10.2 collective-permute-done
  758.1 10.2 collective-permute-done
  770.3 10.2 collective-permute-done
  806.8 10.2 collective-permute-done
  819.0 10.2 collective-permute-done
  831.2 10.2 collective-permute-done
  843.4 10.2 collective-permute-done
  892.1 10.2 collective-permute-done
  1647.8 13.1 add_bitcast_fusion
  1668.5 10.5 collective-permute-done.3
  1743.3 13.1 psum.7
  (592 shorter events, 1238.6 us)
Async XLA Ops:
  2.2 46.1 %collective-permute-start.1 = (bf16[3,2,1024]{2,1,0:T(2,128)(2,1)S(1)}, bf16[3,2,1024]{2,1,0:T(2,128)(2,1)S(1)}, u32[]{:S(2)}, u32[]{:S(2)}) collective-permute-start(bf16[3,2,1024]{2,1,0:T(2,128)(2,1)S(1)} %pad_maximum_fusion.5), channel_id=1, source_target_pairs={{0,4},{4,8},{8,12},{12,16},{16,20},{20,24},{24,28},{28,32},{32,36}... | collective-permute-start | bytes 36872 | tf_op jit(solution)/shard_map/ppermute | solution.py:24
  11.5 1653.5 %collective-permute-start.2 = (bf16[128,8,128]{2,0,1:T(8,128)(2,1)}, bf16[128,8,128]{2,0,1:T(8,128)(2,1)}, u32[]{:S(2)}, u32[]{:S(2)}) collective-permute-start(bf16[128,8,128]{2,0,1:T(8,128)(2,1)} %pad_maximum_fusion.4), channel_id=1, source_target_pairs={{508,0},{0,4},{4,8},{8,12},{12,16},{16,20},{20,24},{24,28},{28,32}... | collective-permute-start | bytes 786440 | tf_op jit(solution)/shard_map/ppermute | solution.py:30
  110.9 12.1 collective-permute-start
  123.1 12.1 collective-permute-start
  135.3 12.1 collective-permute-start
  147.5 12.1 collective-permute-start
  184.0 12.1 collective-permute-start
  196.2 12.1 collective-permute-start
  208.3 12.1 collective-permute-start
  220.5 12.1 collective-permute-start
  232.7 12.1 collective-permute-start
  269.2 12.1 collective-permute-start
  281.4 12.1 collective-permute-start
  293.6 12.1 collective-permute-start
  305.7 12.1 collective-permute-start
  342.3 12.1 collective-permute-start
  354.4 12.1 collective-permute-start
  366.6 12.1 collective-permute-start
  378.8 12.1 collective-permute-start
  415.3 12.1 collective-permute-start
  427.5 12.1 collective-permute-start
  439.7 12.1 collective-permute-start
  451.8 12.1 collective-permute-start
  464.0 12.1 collective-permute-start
  500.5 12.1 collective-permute-start
  512.7 12.1 collective-permute-start
  524.9 12.1 collective-permute-start
  537.1 12.1 collective-permute-start
  573.6 12.1 collective-permute-start
  585.8 12.1 collective-permute-start
  597.9 12.1 collective-permute-start
  610.1 12.1 collective-permute-start
  646.6 12.1 collective-permute-start
  658.8 12.1 collective-permute-start
  671.0 12.1 collective-permute-start
  683.2 12.1 collective-permute-start
  695.3 12.1 collective-permute-start
  731.9 12.1 collective-permute-start
  744.0 12.1 collective-permute-start
  1663.1 15.9 collective-permute-start.3
  1665.0 16.8 collective-permute-start.4
  1679.0 14.7 collective-permute-start.5
  1681.8 15.9 collective-permute-start.6
  1693.7 14.7 collective-permute-start.7
  1697.7 18.0 %collective-permute-start.8 = (bf16[128,8,128]{2,0,1:T(8,128)(2,1)S(1)}, bf16[128,8,128]{2,0,1:T(8,128)(2,1)S(1)}, u32[]{:S(2)}, u32[]{:S(2)}) collective-permute-start(bf16[128,8,128]{2,0,1:T(8,128)(2,1)S(1)} %collective-permute-done.6), channel_id=1, source_target_pairs={{508,0},{0,4},{4,8},{8,12},{12,16},{16,20},{20,24},{24,28},{28,32}... | collective-permute-start | bytes 786440 | tf_op jit(solution)/shard_map/ppermute | solution.py:30
  1708.4 16.9 collective-permute-start.9
  1715.6 17.9 %collective-permute-start.10 = (bf16[128,8,128]{2,0,1:T(8,128)(2,1)S(1)}, bf16[128,8,128]{2,0,1:T(8,128)(2,1)S(1)}, u32[]{:S(2)}, u32[]{:S(2)}) collective-permute-start(bf16[128,8,128]{2,0,1:T(8,128)(2,1)S(1)} %collective-permute-done.8), channel_id=1, source_target_pairs={{508,0},{0,4},{4,8},{8,12},{12,16},{16,20},{20,24},{24,28},{28,32}... | collective-permute-start | bytes 786440 | tf_op jit(solution)/shard_map/ppermute | solution.py:30
  1725.3 17.5 collective-permute-start.11
  (104 other events, 2968.0 us)
where the time goes:
time: 1760 us
  waiting for transfers between devices  1350 us (77%)
  starting transfers between devices  271 us (15%)
  matrix products  75.5 us (4%)
  local copies, waits for them, and re-layouts  29.3 us (2%)
    ppermute x128, waiting for transfers between devices, passed_along(): lax.ppermute(value, axis, [(source, source + steps) for source in range(f...  1300 us
    ppermute x128, starting transfers between devices, passed_along(): lax.ppermute(value, axis, [(source, source + steps) for source in range(f...  246 us
    ppermute x10, waiting for transfers between devices, shifted(): return lax.ppermute(block, axis, route)  52 us
  transfers between devices with their start and end apart: 138, of which 136 were waited for; matrix products, arithmetic and copies ran while one was open for 6% of the time, Pallas kernels for 0%

commit v1 on v0

v1 whole, which is shorter than its diff:
```python
import math

import jax
import jax.numpy as jnp
from jax import lax
from jax.experimental import pallas as pl
from jax.experimental.pallas import tpu as pltpu
from jax.sharding import PartitionSpec as P

HEAD_DIM = 128
MODES = 16
TOK = 128
WIDTH = 1024
HEADS = WIDTH // HEAD_DIM
LANES = 128
ROWS = WIDTH // LANES
NX, NZ, NQ = 4, 8, 4
N_CTX = NX * NZ * NQ

orig_window = 8192.0
rope_base = 10000.0
yarn_factor = 128.0
norm_eps = 1e-05
f32 = jnp.float32
bf16 = jnp.bfloat16


def call(kernel, out_shape, args, scratch=(), smem=(), flops=1000000):
    specs = [
        pl.BlockSpec(memory_space=pltpu.SMEM if i in smem else pltpu.VMEM)
        for i in range(len(args))
    ]
    single = not isinstance(out_shape, (list, tuple))
    outs = pl.BlockSpec(memory_space=pltpu.VMEM)
    return pl.pallas_call(
        kernel,
        out_shape=out_shape,
        in_specs=specs,
        out_specs=outs if single else [outs] * len(out_shape),
        scratch_shapes=list(scratch),
        compiler_params=pltpu.CompilerParams(vmem_limit_bytes=24 * 1024 * 1024),
        cost_estimate=pl.CostEstimate(flops=flops, bytes_accessed=1000000, transcendentals=0),
    )(*args)


def sds(shape, dtype):
    return jax.ShapeDtypeStruct(shape, dtype)


def head_freqs(head_dim):
    half_dim = head_dim // 2
    base_freq = jnp.power(rope_base, -2.0 * jnp.arange(half_dim, dtype=f32) / head_dim)
    wave_ratio = orig_window * base_freq / (2.0 * math.pi)
    ramp_mix = jnp.clip((wave_ratio - 1.0) / 31.0, 0.0, 1.0)
    return base_freq * ramp_mix + base_freq / yarn_factor * (1.0 - ramp_mix)


def lane_block(j):
    return slice(j * LANES, (j + 1) * LANES)


def tok_rows(t):
    return pl.ds(pl.multiple_of(t * ROWS, ROWS), ROWS)


def tree_sum(items):
    items = list(items)
    while len(items) > 1:
        items = [
            items[i] + items[i + 1] if i + 1 < len(items) else items[i]
            for i in range(0, len(items), 2)
        ]
    return items[0]


def modes_of(ref):
    return [ref[m * ROWS : (m + 1) * ROWS, :] for m in range(MODES)]


def rotate_kernel(q_ref, k_ref, cos_ref, sin_ref, qo_ref, ko_ref):
    cosine = cos_ref[...]
    sine = sin_ref[...]
    for src, dst in ((k_ref, ko_ref), (q_ref, qo_ref)):
        for h in range(HEADS):
            x = src[:, lane_block(h)].astype(f32)
            dst[:, lane_block(h)] = (x * cosine + pltpu.roll(x, HEAD_DIM // 2, 1) * sine).astype(bf16)


def local_kernel(
    q_ref, k_ref, v_ref, taps_ref, res_ref, rate_ref,
    l_ref, fq_ref, f0_ref, rr_ref, gg_ref, tp_ref, edge_ref,
    qs, ks, vs, rs,
):
    for part in range(MODES // 8):
        for j in range(ROWS):
            rows = pl.ds(part * 8 * ROWS + j, 8, stride=ROWS)
            rr_ref[rows, :] = rate_ref[part * 8 : part * 8 + 8, lane_block(j)]
            rs[rows, :] = res_ref[part * 8 : part * 8 + 8, lane_block(j)]
    for a in range(3):
        for j in range(ROWS):
            tp_ref[pl.ds(a * 3 * ROWS + j, 3, stride=ROWS), :] = taps_ref[a, :, lane_block(j)]
    for src, dst in ((k_ref, ks), (v_ref, vs), (q_ref, qs)):
        for g in range(TOK // 16):
            block = src[g * 16 : (g + 1) * 16, :].astype(f32)
            for s in range(2):
                for j in range(ROWS):
                    dst[pl.ds((g * 16 + s * 8) * ROWS + j, 8, stride=ROWS), :] = block[
                        s * 8 : s * 8 + 8, lane_block(j)
                    ]
    for i, src in enumerate((ks, vs, qs)):
        edge_ref[i * 2 * ROWS : (i + 1) * 2 * ROWS, :] = src[0 : 2 * ROWS, :]
    rate = rr_ref[...]
    x = 2.0 * rate
    series = x * (1.0 - x / 2.0 * (1.0 - x / 3.0 * (1.0 - x / 4.0 * (
        1.0 - x / 5.0 * (1.0 - x / 6.0 * (1.0 - x / 7.0))))))
    gg_ref[...] = rs[...] * jnp.sqrt(series)
    rs[...] = jnp.exp(-rate)
    decay = modes_of(rs)
    gain = modes_of(gg_ref)
    tap = [tp_ref[i * ROWS : (i + 1) * ROWS, :] for i in range(9)]
    unroll = 6

    def step(it, carry):
        state = list(carry)
        for o in range(unroll):
            t = it * unroll + 2 + o
            now, one, two = tok_rows(t), tok_rows(t - 1), tok_rows(t - 2)
            feat_k = tap[3] * ks[now, :] + tap[4] * ks[one, :] + tap[5] * ks[two, :]
            feat_v = tap[6] * vs[now, :] + tap[7] * vs[one, :] + tap[8] * vs[two, :]
            fq_ref[now, :] = tap[0] * qs[now, :] + tap[1] * qs[one, :] + tap[2] * qs[two, :]
            mixed = feat_k * feat_v
            state = [decay[m] * state[m] + gain[m] * mixed for m in range(MODES)]
            l_ref[now, :] = tree_sum(state)
        return tuple(state)

    zero = jnp.zeros((ROWS, LANES), f32)
    state = lax.fori_loop(0, (TOK - 2) // unroll, step, (zero,) * MODES)
    for m in range(MODES):
        f0_ref[m * ROWS : (m + 1) * ROWS, :] = state[m]


def edge_kernel(halo_ref, edge_ref, tp_ref, rr_ref, gg_ref, f0_ref, f_ref, em_ref, hs):
    halo = halo_ref[...].astype(f32)
    for j in range(ROWS):
        hs[pl.ds(j, 8, stride=ROWS), :] = halo[:, lane_block(j)]

    def row(ref, i):
        return ref[i * ROWS : (i + 1) * ROWS, :]

    tap = [row(tp_ref, i) for i in range(9)]

    def feats(i, base):
        prev2, prev1 = row(hs, 2 * i), row(hs, 2 * i + 1)
        tok0, tok1 = row(edge_ref, 2 * i), row(edge_ref, 2 * i + 1)
        w = tap[base : base + 3]
        return (
            w[0] * tok0 + w[1] * prev1 + w[2] * prev2,
            w[0] * tok1 + w[1] * tok0 + w[2] * prev1,
        )

    k0, k1 = feats(0, 3)
    v0, v1 = feats(1, 6)
    q0, q1 = feats(2, 0)
    m0, m1 = k0 * v0, k1 * v1
    for i, value in enumerate((m0, m1, q0, q1)):
        em_ref[i * ROWS : (i + 1) * ROWS, :] = value
    for i in range(MODES // 2):
        both = []
        for m in (2 * i, 2 * i + 1):
            rate, gain = row(rr_ref, m), row(gg_ref, m)
            both.append(
                row(f0_ref, m)
                + gain * (jnp.exp(rate * -127.0) * m0 + jnp.exp(rate * -126.0) * m1)
            )
        f_ref[i * 2 * ROWS : (i + 1) * 2 * ROWS, :] = jnp.concatenate(both, axis=0).astype(bf16)


def weight(rate, span, steps):
    factor = jnp.exp(rate * (jnp.maximum(steps, 0) * -span).astype(f32))
    return jnp.where(steps >= 0, factor, 0.0)


def quad_kernel(idx_ref, fq_ref, rr_ref, t_ref, before_ref):
    q = idx_ref[2]
    rate = rr_ref[...]
    f = [fq_ref[i * LANES : (i + 1) * LANES, :].astype(f32) for i in range(NQ)]
    d1 = jnp.exp(rate * -float(TOK))
    total = f[0]
    for i in range(1, NQ):
        total = d1 * total + f[i]
    total = total.astype(bf16)
    for i in range(NZ):
        t_ref[i] = total
    before_ref[...] = tree_sum([weight(rate, TOK, q - 1 - i) * f[i] for i in range(NQ - 1)])


def z_kernel(idx_ref, tz_ref, rr_ref, u_ref, before_ref):
    z = idx_ref[1]
    rate = rr_ref[...]
    d = jnp.exp(rate * -float(TOK * NQ))
    total = tz_ref[0].astype(f32)
    before = jnp.zeros_like(total)
    for i in range(1, NZ):
        before = jnp.where(z == i, total, before)
        total = d * total + tz_ref[i].astype(f32)
    total = total.astype(bf16)
    for i in range(NX):
        u_ref[i] = total
    before_ref[...] = before


def out_kernel(idx_ref, ux_ref, zb_ref, qb_ref, rr_ref, gg_ref, em_ref, l_ref, fq_ref, out_ref, cs, ys):
    x, z, q = idx_ref[0], idx_ref[1], idx_ref[2]
    rate = rr_ref[...]
    d = jnp.exp(rate * -float(TOK * NQ * NZ))
    carry = jnp.zeros_like(rate)
    running = ux_ref[0].astype(f32)
    for i in range(1, NX):
        carry = jnp.where(x == i, running, carry)
        if i < NX - 1:
            running = d * running + ux_ref[i].astype(f32)
    group = zb_ref[...] + jnp.exp(rate * (z * -(TOK * NQ)).astype(f32)) * carry
    own = qb_ref[...] + jnp.exp(rate * (q * -TOK).astype(f32)) * group
    decay_all = jnp.exp(-rate)
    gain_all = gg_ref[...]

    def tile(value, m):
        return value[m * ROWS : (m + 1) * ROWS, :]

    decay = [tile(decay_all, m) for m in range(MODES)]
    m0, m1, q0, q1 = [em_ref[i * ROWS : (i + 1) * ROWS, :] for i in range(4)]
    state = [decay[m] * tile(own, m) + tile(gain_all, m) * m0 for m in range(MODES)]
    ys[0:ROWS, :] = q0 * tree_sum(state)
    state = [decay[m] * state[m] + tile(gain_all, m) * m1 for m in range(MODES)]
    ys[ROWS : 2 * ROWS, :] = q1 * tree_sum(state)
    for m in range(MODES):
        cs[m * ROWS : (m + 1) * ROWS, :] = tile(decay_all, m)
    unroll = 6

    def step(it, carry_now):
        state = list(carry_now)
        for o in range(unroll):
            now = tok_rows(it * unroll + 2 + o)
            state = [cs[m * ROWS : (m + 1) * ROWS, :] * state[m] for m in range(MODES)]
            ys[now, :] = fq_ref[now, :] * (l_ref[now, :] + tree_sum(state))
        return tuple(state)

    lax.fori_loop(0, (TOK - 2) // unroll, step, tuple(state))
    for g in range(TOK // 16):
        for j in range(ROWS):
            halves = [
                ys[pl.ds((g * 16 + s * 8) * ROWS + j, 8, stride=ROWS), :] for s in range(2)
            ]
            out_ref[g * 16 : (g + 1) * 16, lane_block(j)] = jnp.concatenate(halves, axis=0).astype(bf16)


def weights_kernel(mask_ref, q_ref, k0_ref, k1_ref, k2_ref, k3_ref, k4_ref, k5_ref, w_ref, inv_ref):
    yarn_scale = 0.1 * math.log(yarn_factor) + 1.0
    coef = yarn_scale * yarn_scale / math.sqrt(HEAD_DIM) * math.log2(math.e)
    pieces = (k0_ref, k1_ref, k2_ref, k3_ref, k4_ref, k5_ref)
    shape = (TOK, TOK)
    causal = lax.broadcasted_iota(jnp.int32, shape, 1) <= lax.broadcasted_iota(jnp.int32, shape, 0)
    lane = lax.broadcasted_iota(jnp.int32, (TOK, LANES), 1)
    inverse = jnp.zeros((TOK, LANES), f32)
    for h in range(HEADS):
        query = q_ref[:, lane_block(h)]
        scores = []
        for i, piece in enumerate(pieces):
            s = lax.dot_general(
                query, piece[:, lane_block(h)], (((1,), (1,)), ((), ())), preferred_element_type=f32
            ) * coef
            allowed = mask_ref[i] == 1
            visible = (causal & allowed) if i == 0 else jnp.broadcast_to(allowed, shape)
            scores.append(jnp.where(visible, s, -1e30))
        top = scores[0]
        for s in scores[1:]:
            top = jnp.maximum(top, s)
        top = jnp.max(top, axis=1, keepdims=True)
        total = None
        for i, s in enumerate(scores):
            w = jnp.exp2(s - top)
            total = w if total is None else total + w
            w_ref[h, :, lane_block(i)] = w.astype(bf16)
        total = jnp.sum(total, axis=1, keepdims=True)
        inverse = jnp.where(lane == h, 1.0 / total, inverse)
    inv_ref[...] = inverse


def attend_kernel(w_ref, inv_ref, v0_ref, v1_ref, v2_ref, v3_ref, v4_ref, v5_ref, a_ref, sq_ref):
    pieces = (v0_ref, v1_ref, v2_ref, v3_ref, v4_ref, v5_ref)
    inverse = inv_ref[...]
    squares = None
    for h in range(HEADS):
        acc = None
        for i, piece in enumerate(pieces):
            part = jnp.dot(w_ref[h, :, lane_block(i)], piece[:, lane_block(h)], preferred_element_type=f32)
            acc = part if acc is None else acc + part
        acc = acc * inverse[:, h : h + 1]
        a_ref[:, lane_block(h)] = acc
        squares = acc * acc if squares is None else squares + acc * acc
    sums = jnp.sum(squares, axis=1, keepdims=True)
    shape = (TOK, TOK)
    diag = lax.broadcasted_iota(jnp.int32, shape, 1) == lax.broadcasted_iota(jnp.int32, shape, 0)
    sq_ref[...] = jnp.sum(jnp.where(diag, sums, 0.0), axis=0, keepdims=True)


def norm_kernel(a_ref, sq_ref, gain_ref, out_ref):
    shape = (TOK, TOK)
    diag = lax.broadcasted_iota(jnp.int32, shape, 1) == lax.broadcasted_iota(jnp.int32, shape, 0)
    sums = jnp.sum(jnp.where(diag, sq_ref[...], 0.0), axis=1, keepdims=True)
    scale = lax.rsqrt(sums / float(WIDTH * 4) + norm_eps)
    out_ref[...] = (a_ref[...] * scale * gain_ref[...]).astype(bf16)


def quad_groups():
    return [[g * NQ + q for q in range(NQ)] for g in range(NX * NZ)]


def z_groups():
    return [[(x * NZ + z) * NQ + q for z in range(NZ)] for x in range(NX) for q in range(NQ)]


def x_groups():
    return [[(x * NZ + z) * NQ + q for x in range(NX)] for z in range(NZ) for q in range(NQ)]


def ahead(value, steps):
    return lax.ppermute(value, "ctx", [(i, (i + steps) % N_CTX) for i in range(N_CTX)])


def core_swap(value):
    return lax.ppermute(value, "ctx", [(i, i ^ 1) for i in range(N_CTX)])


def window(value):
    extra = lax.ppermute(
        value, "ctx", [(i, (i + (5 if i % 2 else 1)) % N_CTX) for i in range(N_CTX)]
    )
    two = ahead(value, 2)
    four = ahead(value, 4)
    return [value, two, four, core_swap(two), core_swap(four), extra]


def local(
    hyena_q, hyena_k, hyena_v, short_taps, residues, rates, queries, keys, offsets, block_mask, out_gain
):
    me = lax.axis_index("ctx")
    idx = jnp.stack([me // (NZ * NQ), (me // NQ) % NZ, me % NQ]).astype(jnp.int32)
    rim = jnp.concatenate(
        [hyena_k[TOK - 2 :], hyena_v[TOK - 2 :], hyena_q[TOK - 2 :], hyena_q[TOK - 2 :]], axis=0
    )
    halo = lax.ppermute(rim, "ctx", [(i, i + 1) for i in range(N_CTX - 1)])

    angles = (offsets[me] + jnp.arange(TOK, dtype=jnp.int32)).astype(f32)[:, None] * head_freqs(HEAD_DIM)[None, :]
    cosine, sine = jnp.cos(angles), jnp.sin(angles)
    q_rot, k_rot = call(
        rotate_kernel,
        [sds((TOK, WIDTH), bf16)] * 2,
        (
            queries,
            keys,
            jnp.concatenate([cosine, cosine], axis=1),
            jnp.concatenate([-sine, sine], axis=1),
        ),
    )
    key_pieces = window(k_rot)

    big, small = sds((TOK * ROWS, LANES), f32), sds((MODES * ROWS, LANES), f32)
    l_rest, feat_q, f0, rr, gg, tp, edge = call(
        local_kernel,
        [big, big, small, small, small, sds((9 * ROWS, LANES), f32), sds((6 * ROWS, LANES), f32)],
        (hyena_q, hyena_k, hyena_v, short_taps, residues, rates),
        scratch=[pltpu.VMEM((TOK * ROWS, LANES), f32)] * 3 + [pltpu.VMEM((MODES * ROWS, LANES), f32)],
    )
    state, em = call(
        edge_kernel,
        [sds((MODES * ROWS, LANES), bf16), sds((4 * ROWS, LANES), f32)],
        (halo, edge, tp, rr, gg, f0),
        scratch=[pltpu.VMEM((8 * ROWS, LANES), f32)],
    )
    quad = lax.all_gather(state, "ctx", axis_index_groups=quad_groups(), tiled=True)
    group, quad_before = call(
        quad_kernel, [sds((NZ, MODES * ROWS, LANES), bf16), small], (idx, quad, rr), smem=(0,)
    )
    along_z = lax.all_to_all(group, "ctx", 0, 0, tiled=True, axis_index_groups=z_groups())
    column, z_before = call(
        z_kernel, [sds((NX, MODES * ROWS, LANES), bf16), small], (idx, along_z, rr), smem=(0,)
    )
    along_x = lax.all_to_all(column, "ctx", 0, 0, tiled=True, axis_index_groups=x_groups())
    hyena_out = call(
        out_kernel,
        sds((TOK, WIDTH), bf16),
        (idx, along_x, z_before, quad_before, rr, gg, em, l_rest, feat_q),
        scratch=[pltpu.VMEM((MODES * ROWS, LANES), f32), pltpu.VMEM((TOK * ROWS, LANES), f32)],
        smem=(0,),
    )
    value_pieces = window(hyena_out)

    order = jnp.where(
        me % 2 == 0, jnp.array([0, 2, 4, 1, 3, 5], jnp.int32), jnp.array([0, 2, 4, 3, 5, 1], jnp.int32)
    )
    weights, inverse = call(
        weights_kernel,
        [sds((HEADS, TOK, 6 * TOK), bf16), sds((TOK, LANES), f32)],
        (block_mask[0][order], q_rot, *key_pieces),
        smem=(0,),
    )
    attended, squares = call(
        attend_kernel,
        [sds((TOK, WIDTH), f32), sds((1, TOK), f32)],
        (weights, inverse, *value_pieces),
    )
    total = lax.psum(squares, "ch")
    attn_out = call(norm_kernel, sds((TOK, WIDTH), bf16), (attended, total, out_gain[None, :]))
    return (hyena_out, attn_out)


def solution(mesh):
    return jax.shard_map(
        local,
        mesh=mesh,
        in_specs=(
            P("ctx", "ch"),
            P("ctx", "ch"),
            P("ctx", "ch"),
            P(None, None, "ch"),
            P(None, "ch"),
            P(None, "ch"),
            P("ctx", "ch"),
            P("ctx", "ch"),
            P(),
            P("ctx", None),
            P("ch"),
        ),
        out_specs=(P("ctx", "ch"), P("ctx", "ch")),
        check_vma=False,
    )
```

time: 1760 us -> 120 us (0.07)
  waiting for transfers between devices: 1350 us -> 30.2 us
  starting transfers between devices: 271 us -> 46.6 us
  matrix products: 75.5 us -> 0 us
  local copies, waits for them, and re-layouts: 29.3 us -> 8.78 us
    ppermute x138 -> x11, waiting for transfers between devices: 1350 us -> 19.6 us  [the longest x1 8.1 us: local(): halo = lax.ppermute(rim, 'ctx', [(i, i + 1) for i in range(N_CTX - 1)])]
    ppermute x138 -> x11, starting transfers between devices: 271 us -> 34.9 us  [the longest x4 14.5 us: core_swap(): return lax.ppermute(value, 'ctx', [(i, i ^ 1) for i in range(N_CTX)])]
    dot_general x17 -> x0, matrix products: 75.5 us -> none  [the longest x1 29.6 us: stretch_local(): jnp.einsum('tsc,bsc->btc', toeplitz, blocks, precision=highest)]
  transfers between devices with their start and end apart: 138 -> 13, of which waited for: 136 -> 6; matrix products, arithmetic and copies ran while one was open for 6% -> 2% of each run, Pallas kernels for 0% -> 6%
where the time goes in v1:
time: 120 us; the launch traced here: 118 us
  starting transfers between devices  46.6 us (39%)
  waiting for transfers between devices  30.2 us (25%)
  blocking collectives  19.3 us (16%)
  Pallas kernels  10.6 us (9%)
  local copies, waits for them, and re-layouts  8.78 us (7%)
    ppermute x4, starting transfers between devices, core_swap(): return lax.ppermute(value, 'ctx', [(i, i ^ 1) for i in range(N_CTX)])  14.5 us
    ppermute x4, starting transfers between devices, ahead(): lax.ppermute(value, 'ctx', [(i, (i + steps) % N_CTX) for i in range(N_CTX)])  14.5 us
    all_to_all x1, waiting for transfers between devices, local(): lax.all_to_all(group, 'ctx', 0, 0, tiled=True, axis_index_groups=z_groups())  10.6 us
    pallas_call x9, Pallas kernels, call(): pl.pallas_call(kernel, out_shape=out_shape, in_specs=specs, out_specs=out...  10.6 us
    psum x1, blocking collectives, local(): total = lax.psum(squares, 'ch')  10 us
    all_gather x1, blocking collectives, local(): lax.all_gather(state, 'ctx', axis_index_groups=quad_groups(), tiled=True)  9.33 us
    ppermute x1, waiting for transfers between devices, local(): halo = lax.ppermute(rim, 'ctx', [(i, i + 1) for i in range(N_CTX - 1)])  8.1 us
    all_to_all x1, starting transfers between devices, local(): lax.all_to_all(group, 'ctx', 0, 0, tiled=True, axis_index_groups=z_groups())  6.85 us
  transfers between devices with their start and end apart: 13, of which 6 were waited for; matrix products, arithmetic and copies ran while one was open for 2% of the time, Pallas kernels for 6%

profile of v1, /device:TPU:6, one launch (start us, length us, event | category | flops | bytes accessed | tf_op | source)
XLA Modules:
  0.0 117.7 jit_solution(10135062066709477898)
XLA Ops:
  0.6 0.0 copy-start
  0.7 0.7 slice.12
  1.4 0.7 slice.10
  2.1 0.7 slice.11
  2.9 1.9 %collective-permute-start = (bf16[8,1024]{1,0:T(8,128)(2,1)S(1)}, bf16[8,1024]{1,0:T(8,128)(2,1)S(1)}, u32[]{:S(2)}, u32[]{:S(2)}) collective-permute-start(bf16[8,1024]{1,0:T(8,128)(2,1)S(1)} %pad_maximum_fusion.2), channel_id=1, source_target_pairs={{0,4},{4,8},{8,12},{12,16},{16,20},{20,24},{24,28},{28,32},{32,36}... | collective-permute-start | bytes 49160 | tf_op jit(solution)/shard_map/ppermute | solution.py:352
  4.8 0.1 pad_add_fusion.idx_ref
  4.9 0.9 copy-done.2
  5.9 0.9 copy-done.3
  6.8 0.9 copy-done.4
  7.8 0.8 copy-done.7
  8.6 0.8 copy-done.8
  9.4 0.8 copy-done.9
  10.2 1.8 %shard_map.140 = (f32[1024,128]{1,0:T(8,128)S(1)}, f32[1024,128]{1,0:T(8,128)S(1)}, f32[128,128]{1,0:T(8,128)S(1)}, f32[128,128]{1,0:T(8,128)S(1)}, f32[128,128]...) custom-call(bf16[128,1024]{1,0:T(8,128)(2,1)S(1)} %copy-done.2, bf16[128,1024]{1,0:T(8,128)(2,1)S(1)} %copy-done.4, ...), custom_call_target="tpu_custom_call" | custom-call | flops 1000000 | bytes 1000000 | tf_op jit(solution)/shard_map/pallas_call | solution.py:35
  12.1 8.1 %collective-permute-done.halo_ref = bf16[8,1024]{1,0:T(8,128)(2,1)S(1)} collective-permute-done((bf16[8,1024]{1,0:T(8,128)(2,1)S(1)}, bf16[8,1024]{1,0:T(8,128)(2,1)S(1)}, u32[]{:S(2)}, u32[]{:S(2)}) %collective-permute-start) | collective-permute-done | bytes 16416 | tf_op jit(solution)/shard_map/ppermute | solution.py:352
  20.2 9.3 %all_gather.3.fq_ref = bf16[512,128]{1,0:T(8,128)(2,1)S(1)} all-gather(bf16[128,128]{1,0:T(8,128)(2,1)S(1)} %get-tuple-element.26), channel_id=1, replica_groups={{0,4,8,12},{16,20,24,28},{32,36,40,44},{48,52,56,60},{64,68,72,76},{80,..., dimensions={0}, use_global_device_ids=true | all-gather | bytes 163840 | tf_op jit(solution)/shard_map/all_gather | solution.py:381
  29.6 1.3 %shard_map.142 = (bf16[8,128,128]{2,1,0:T(8,128)(2,1)}, f32[128,128]{1,0:T(8,128)S(1)}) custom-call(s32[3]{0:T(128)S(1)} %pad_add_fusion.idx_ref, bf16[512,128]{1,0:T(8,128)(2,1)S(1)} %all_gather.3.fq_ref, f32[128,128]{1,0:T(8,128)S(1)} %get-tuple-element.23.rr_ref), custom_call_target="tpu_custom_call" | custom-call | flops 1000000 | bytes 1000000 | tf_op jit(solution)/shard_map/pallas_call | solution.py:35
  30.9 6.8 %all-to-all-start = ((bf16[8,128,128]{2,1,0:T(8,128)(2,1)}), bf16[8,128,128]{2,1,0:T(8,128)(2,1)S(1)}, u32[]{:S(2)}, u32[]{:S(2)}) async-start(bf16[8,128,128]{2,1,0:T(8,128)(2,1)} %get-tuple-element.27), calls=%async_computation | async-start | bytes 524288 | tf_op jit(solution)/shard_map/all_to_all | solution.py:385
  37.7 0.6 dynamic_slice.3
  38.3 0.7 add_convert_fusion
  39.0 0.3 fusion
  39.3 10.6 %all-to-all-done.tz_ref = bf16[8,128,128]{2,1,0:T(8,128)(2,1)S(1)} async-done(((bf16[8,128,128]{2,1,0:T(8,128)(2,1)}), bf16[8,128,128]{2,1,0:T(8,128)(2,1)S(1)}, u32[]{:S(2)}, u32[]{:S(2)}) %all-to-all-start) | async-done | bytes 262176 | tf_op jit(solution)/shard_map/all_to_all | solution.py:385
  49.9 1.3 %shard_map.143 = (bf16[4,128,128]{2,1,0:T(8,128)(2,1)}, f32[128,128]{1,0:T(8,128)S(1)}) custom-call(s32[3]{0:T(128)S(1)} %pad_add_fusion.idx_ref, bf16[8,128,128]{2,1,0:T(8,128)(2,1)S(1)} %all-to-all-done.tz_ref, f32[128,128]{1,0:T(8,128)S(1)} %get-tuple-element.23.rr_ref), custom_call_target="tpu_custom_call" | custom-call | flops 1000000 | bytes 1000000 | tf_op jit(solution)/shard_map/pallas_call | solution.py:35
  51.2 4.9 %all-to-all-start.1 = ((bf16[4,128,128]{2,1,0:T(8,128)(2,1)}), bf16[4,128,128]{2,1,0:T(8,128)(2,1)S(1)}, u32[]{:S(2)}, u32[]{:S(2)}) async-start(bf16[4,128,128]{2,1,0:T(8,128)(2,1)} %get-tuple-element.28), calls=%async_computation.1 | async-start | bytes 262144 | tf_op jit(solution)/shard_map/all_to_all | solution.py:389
  56.1 0.1 pad_maximum_fusion
  56.2 0.3 shard_map.145
  56.5 1.9 %collective-permute-start.5 = (bf16[128,1024]{1,0:T(8,128)(2,1)S(1)}, bf16[128,1024]{1,0:T(8,128)(2,1)S(1)}, u32[]{:S(2)}, u32[]{:S(2)}) collective-permute-start(bf16[128,1024]{1,0:T(8,128)(2,1)S(1)} %get-tuple-element.35.k0_ref), channel_id=1, source_target_pairs={{0,4},{4,24},{8,12},{12,32},{16,20},{20,40},{24,28},{28,48},{32,36... | collective-permute-start | bytes 786440 | tf_op jit(solution)/shard_map/ppermute | solution.py:336
  58.4 2.5 %collective-permute-start.2 = (bf16[128,1024]{1,0:T(8,128)(2,1)S(1)}, bf16[128,1024]{1,0:T(8,128)(2,1)S(1)}, u32[]{:S(2)}, u32[]{:S(2)}) collective-permute-start(bf16[128,1024]{1,0:T(8,128)(2,1)S(1)} %get-tuple-element.35.k0_ref), channel_id=1, source_target_pairs={{0,16},{4,20},{8,24},{12,28},{16,32},{20,36},{24,40},{28,44},{32,4... | collective-permute-start | bytes 786440 | tf_op jit(solution)/shard_map/ppermute | solution.py:328
  60.9 3.7 %collective-permute-start.1 = (bf16[128,1024]{1,0:T(8,128)(2,1)S(1)}, bf16[128,1024]{1,0:T(8,128)(2,1)S(1)}, u32[]{:S(2)}, u32[]{:S(2)}) collective-permute-start(bf16[128,1024]{1,0:T(8,128)(2,1)S(1)} %get-tuple-element.35.k0_ref), channel_id=1, source_target_pairs={{0,8},{4,12},{8,16},{12,20},{16,24},{20,28},{24,32},{28,36},{32,40... | collective-permute-start | bytes 786440 | tf_op jit(solution)/shard_map/ppermute | solution.py:328
  64.6 0.0 all-to-all-done.1.ux_ref
  64.6 2.1 %shard_map.144.v0_ref = bf16[128,1024]{1,0:T(8,128)(2,1)} custom-call(s32[3]{0:T(128)S(1)} %pad_add_fusion.idx_ref, bf16[4,128,128]{2,1,0:T(8,128)(2,1)S(1)} %all-to-all-done.1.ux_ref, f32[128,128]{1,0:T(8,128)S(1)} %get-tuple-element.29.zb_ref, f32[128,128]{1,0:T(8,128)S(1)} %get-tuple-element.30.qb_ref, f32[128,128]{1,0:T(8,128)S(1)} %get-tuple-element.23.rr_ref, ...), custom_call_target="tpu_custom_call" | custom-call | flops 1000000 | bytes 1000000 | tf_op jit(solution)/shard_map/pallas_call | solution.py:35
  66.7 2.0 %collective-permute-start.7 = (bf16[128,1024]{1,0:T(8,128)(2,1)}, bf16[128,1024]{1,0:T(8,128)(2,1)S(1)}, u32[]{:S(2)}, u32[]{:S(2)}) collective-permute-start(bf16[128,1024]{1,0:T(8,128)(2,1)} %shard_map.144.v0_ref), channel_id=1, source_target_pairs={{0,16},{4,20},{8,24},{12,28},{16,32},{20,36},{24,40},{28,44},{32,4... | collective-permute-start | bytes 786440 | tf_op jit(solution)/shard_map/ppermute | solution.py:328
  68.8 6.3 %collective-permute-start.6 = (bf16[128,1024]{1,0:T(8,128)(2,1)}, bf16[128,1024]{1,0:T(8,128)(2,1)S(1)}, u32[]{:S(2)}, u32[]{:S(2)}) collective-permute-start(bf16[128,1024]{1,0:T(8,128)(2,1)} %shard_map.144.v0_ref), channel_id=1, source_target_pairs={{0,8},{4,12},{8,16},{12,20},{16,24},{20,28},{24,32},{28,36},{32,40... | collective-permute-start | bytes 786440 | tf_op jit(solution)/shard_map/ppermute | solution.py:328
  75.1 3.7 %collective-permute-done.2.k2_ref = bf16[128,1024]{1,0:T(8,128)(2,1)S(1)} collective-permute-done((bf16[128,1024]{1,0:T(8,128)(2,1)S(1)}, bf16[128,1024]{1,0:T(8,128)(2,1)S(1)}, u32[]{:S(2)}, u32[]{:S(2)}) %collective-permute-start.2) | collective-permute-done | bytes 262176 | tf_op jit(solution)/shard_map/ppermute | solution.py:328
  78.8 6.0 %collective-permute-start.4 = (bf16[128,1024]{1,0:T(8,128)(2,1)S(1)}, bf16[128,1024]{1,0:T(8,128)(2,1)S(1)}, u32[]{:S(2)}, u32[]{:S(2)}) collective-permute-start(bf16[128,1024]{1,0:T(8,128)(2,1)S(1)} %collective-permute-done.2.k2_ref), channel_id=1, source_target_pairs={{0,4},{4,0},{8,12},{12,8},{16,20},{20,16},{24,28},{28,24},{32,36},... | collective-permute-start | bytes 786440 | tf_op jit(solution)/shard_map/ppermute | solution.py:332
  84.8 0.0 collective-permute-done.1.k1_ref
  84.8 2.3 %collective-permute-start.3 = (bf16[128,1024]{1,0:T(8,128)(2,1)S(1)}, bf16[128,1024]{1,0:T(8,128)(2,1)S(1)}, u32[]{:S(2)}, u32[]{:S(2)}) collective-permute-start(bf16[128,1024]{1,0:T(8,128)(2,1)S(1)} %collective-permute-done.1.k1_ref), channel_id=1, source_target_pairs={{0,4},{4,0},{8,12},{12,8},{16,20},{20,16},{24,28},{28,24},{32,36},... | collective-permute-start | bytes 786440 | tf_op jit(solution)/shard_map/ppermute | solution.py:332
  87.1 2.1 %collective-permute-start.10 = (bf16[128,1024]{1,0:T(8,128)(2,1)}, bf16[128,1024]{1,0:T(8,128)(2,1)S(1)}, u32[]{:S(2)}, u32[]{:S(2)}) collective-permute-start(bf16[128,1024]{1,0:T(8,128)(2,1)} %shard_map.144.v0_ref), channel_id=1, source_target_pairs={{0,4},{4,24},{8,12},{12,32},{16,20},{20,40},{24,28},{28,48},{32,36... | collective-permute-start | bytes 786440 | tf_op jit(solution)/shard_map/ppermute | solution.py:336
  89.1 0.6 collective-permute-done.7.v2_ref
  89.7 4.3 %collective-permute-start.9 = (bf16[128,1024]{1,0:T(8,128)(2,1)S(1)}, bf16[128,1024]{1,0:T(8,128)(2,1)S(1)}, u32[]{:S(2)}, u32[]{:S(2)}) collective-permute-start(bf16[128,1024]{1,0:T(8,128)(2,1)S(1)} %collective-permute-done.7.v2_ref), channel_id=1, source_target_pairs={{0,4},{4,0},{8,12},{12,8},{16,20},{20,16},{24,28},{28,24},{32,36},... | collective-permute-start | bytes 786440 | tf_op jit(solution)/shard_map/ppermute | solution.py:332
  94.0 1.7 %collective-permute-done.6.v1_ref = bf16[128,1024]{1,0:T(8,128)(2,1)S(1)} collective-permute-done((bf16[128,1024]{1,0:T(8,128)(2,1)}, bf16[128,1024]{1,0:T(8,128)(2,1)S(1)}, u32[]{:S(2)}, u32[]{:S(2)}) %collective-permute-start.6) | collective-permute-done | bytes 262176 | tf_op jit(solution)/shard_map/ppermute | solution.py:328
  95.7 2.0 %collective-permute-start.8 = (bf16[128,1024]{1,0:T(8,128)(2,1)S(1)}, bf16[128,1024]{1,0:T(8,128)(2,1)S(1)}, u32[]{:S(2)}, u32[]{:S(2)}) collective-permute-start(bf16[128,1024]{1,0:T(8,128)(2,1)S(1)} %collective-permute-done.6.v1_ref), channel_id=1, source_target_pairs={{0,4},{4,0},{8,12},{12,8},{16,20},{20,16},{24,28},{28,24},{32,36},... | collective-permute-start | bytes 786440 | tf_op jit(solution)/shard_map/ppermute | solution.py:332
  97.8 0.6 gather_fusion
  98.4 2.3 %shard_map.146 = (bf16[8,128,768]{2,1,0:T(8,128)(2,1)S(1)}, f32[128,128]{1,0:T(8,128)S(1)}) custom-call(s32[6]{0:T(128)S(1)} %gather_fusion, bf16[128,1024]{1,0:T(8,128)(2,1)S(1)} %get-tuple-element.34.q_ref, bf16[128,1024]{1,0:T(8,128)(2,1)S(1)} %get-tuple-element.35.k0_ref, bf16[128,1024]{1,0:T(8,128)(2,1)S(1)} %collective-permute-done.1.k1_ref, ...), custom_call_target="tpu_custom_call" | custom-call | flops 1000000 | bytes 1000000 | tf_op jit(solution)/shard_map/pallas_call | solution.py:35
  100.7 5.5 %collective-permute-done.10.v5_ref = bf16[128,1024]{1,0:T(8,128)(2,1)S(1)} collective-permute-done((bf16[128,1024]{1,0:T(8,128)(2,1)}, bf16[128,1024]{1,0:T(8,128)(2,1)S(1)}, u32[]{:S(2)}, u32[]{:S(2)}) %collective-permute-start.10) | collective-permute-done | bytes 262176 | tf_op jit(solution)/shard_map/ppermute | solution.py:336
  106.2 0.0 copy-start.10
  106.2 0.7 shard_map.147
  106.9 10.0 %psum.7.sq_ref = f32[1,128]{1,0:T(1,128)S(1)} all-reduce(f32[1,128]{1,0:T(1,128)S(1)} %get-tuple-element.39), channel_id=1, replica_groups=mesh['ctx'=128,'ch'=4] {'ch'}, use_global_device_ids=true, to_apply=%region_0.1 | all-reduce | flops 128 | bytes 1024 | tf_op jit(solution)/shard_map/psum | solution.py:413
  116.9 0.8 shard_map.148
  (30 shorter events, 0.1 us)
Async XLA Ops:
  0.6 97.1 %copy-start = (s32[1,6]{1,0:T(1,128)S(1)}, s32[1,6]{1,0:T(1,128)}, u32[]{:S(2)}) copy-start(s32[1,6]{1,0:T(1,128)} %param.22) | copy-start | bytes 76
  0.6 37.1 %copy-start.13 = (s32[128]{0:T(128)S(1)}, s32[128]{0:T(128)}, u32[]{:S(2)}) copy-start(s32[128]{0:T(128)} %param.21) | copy-start | bytes 1540
  2.9 17.3 %collective-permute-start = (bf16[8,1024]{1,0:T(8,128)(2,1)S(1)}, bf16[8,1024]{1,0:T(8,128)(2,1)S(1)}, u32[]{:S(2)}, u32[]{:S(2)}) collective-permute-start(bf16[8,1024]{1,0:T(8,128)(2,1)S(1)} %pad_maximum_fusion.2), channel_id=1, source_target_pairs={{0,4},{4,8},{8,12},{12,16},{16,20},{20,24},{24,28},{28,32},{32,36}... | collective-permute-start | bytes 49160 | tf_op jit(solution)/shard_map/ppermute | solution.py:352
  4.9 1.0 copy-start.2
  5.9 0.9 copy-start.3
  6.8 0.9 copy-start.4
  7.8 0.8 copy-start.7
  8.6 0.8 copy-start.8
  9.4 0.8 copy-start.9
  10.2 46.0 %copy-start.5 = (bf16[128,1024]{1,0:T(8,128)(2,1)S(1)}, bf16[128,1024]{1,0:T(8,128)(2,1)}, u32[]{:S(2)}) copy-start(bf16[128,1024]{1,0:T(8,128)(2,1)} %q_ref.3) | copy-start | bytes 786436
  10.2 46.0 %copy-start.6 = (bf16[128,1024]{1,0:T(8,128)(2,1)S(1)}, bf16[128,1024]{1,0:T(8,128)(2,1)}, u32[]{:S(2)}) copy-start(bf16[128,1024]{1,0:T(8,128)(2,1)} %k_ref.3) | copy-start | bytes 786436
  30.9 19.1 %all-to-all-start = ((bf16[8,128,128]{2,1,0:T(8,128)(2,1)}), bf16[8,128,128]{2,1,0:T(8,128)(2,1)S(1)}, u32[]{:S(2)}, u32[]{:S(2)}) async-start(bf16[8,128,128]{2,1,0:T(8,128)(2,1)} %get-tuple-element.27), calls=%async_computation | async-start | bytes 524288 | tf_op jit(solution)/shard_map/all_to_all | solution.py:385
  51.2 46.5 %copy-start.11 = (s32[6]{0:T(128)S(1)}, s32[6]{0:T(128)}, u32[]{:S(2)}) copy-start(s32[6]{0:T(128)} %constant.96.clone) | copy-start | bytes 76
  51.2 46.5 %copy-start.12 = (s32[6]{0:T(128)S(1)}, s32[6]{0:T(128)}, u32[]{:S(2)}) copy-start(s32[6]{0:T(128)} %constant.95.clone) | copy-start | bytes 76
  51.2 13.4 %all-to-all-start.1 = ((bf16[4,128,128]{2,1,0:T(8,128)(2,1)}), bf16[4,128,128]{2,1,0:T(8,128)(2,1)S(1)}, u32[]{:S(2)}, u32[]{:S(2)}) async-start(bf16[4,128,128]{2,1,0:T(8,128)(2,1)} %get-tuple-element.28), calls=%async_computation.1 | async-start | bytes 262144 | tf_op jit(solution)/shard_map/all_to_all | solution.py:389
  56.5 30.5 %collective-permute-start.5 = (bf16[128,1024]{1,0:T(8,128)(2,1)S(1)}, bf16[128,1024]{1,0:T(8,128)(2,1)S(1)}, u32[]{:S(2)}, u32[]{:S(2)}) collective-permute-start(bf16[128,1024]{1,0:T(8,128)(2,1)S(1)} %get-tuple-element.35.k0_ref), channel_id=1, source_target_pairs={{0,4},{4,24},{8,12},{12,32},{16,20},{20,40},{24,28},{28,48},{32,36... | collective-permute-start | bytes 786440 | tf_op jit(solution)/shard_map/ppermute | solution.py:336
  58.4 20.3 %collective-permute-start.2 = (bf16[128,1024]{1,0:T(8,128)(2,1)S(1)}, bf16[128,1024]{1,0:T(8,128)(2,1)S(1)}, u32[]{:S(2)}, u32[]{:S(2)}) collective-permute-start(bf16[128,1024]{1,0:T(8,128)(2,1)S(1)} %get-tuple-element.35.k0_ref), channel_id=1, source_target_pairs={{0,16},{4,20},{8,24},{12,28},{16,32},{20,36},{24,40},{28,44},{32,4... | collective-permute-start | bytes 786440 | tf_op jit(solution)/shard_map/ppermute | solution.py:328
  60.9 23.9 %collective-permute-start.1 = (bf16[128,1024]{1,0:T(8,128)(2,1)S(1)}, bf16[128,1024]{1,0:T(8,128)(2,1)S(1)}, u32[]{:S(2)}, u32[]{:S(2)}) collective-permute-start(bf16[128,1024]{1,0:T(8,128)(2,1)S(1)} %get-tuple-element.35.k0_ref), channel_id=1, source_target_pairs={{0,8},{4,12},{8,16},{12,20},{16,24},{20,28},{24,32},{28,36},{32,40... | collective-permute-start | bytes 786440 | tf_op jit(solution)/shard_map/ppermute | solution.py:328
  66.7 39.5 %copy-start.1 = (bf16[128,1024]{1,0:T(8,128)(2,1)S(1)}, bf16[128,1024]{1,0:T(8,128)(2,1)}, u32[]{:S(2)}) copy-start(bf16[128,1024]{1,0:T(8,128)(2,1)} %shard_map.144.v0_ref) | copy-start | bytes 786436
  66.7 23.0 %collective-permute-start.7 = (bf16[128,1024]{1,0:T(8,128)(2,1)}, bf16[128,1024]{1,0:T(8,128)(2,1)S(1)}, u32[]{:S(2)}, u32[]{:S(2)}) collective-permute-start(bf16[128,1024]{1,0:T(8,128)(2,1)} %shard_map.144.v0_ref), channel_id=1, source_target_pairs={{0,16},{4,20},{8,24},{12,28},{16,32},{20,36},{24,40},{28,44},{32,4... | collective-permute-start | bytes 786440 | tf_op jit(solution)/shard_map/ppermute | solution.py:328
  68.8 27.0 %collective-permute-start.6 = (bf16[128,1024]{1,0:T(8,128)(2,1)}, bf16[128,1024]{1,0:T(8,128)(2,1)S(1)}, u32[]{:S(2)}, u32[]{:S(2)}) collective-permute-start(bf16[128,1024]{1,0:T(8,128)(2,1)} %shard_map.144.v0_ref), channel_id=1, source_target_pairs={{0,8},{4,12},{8,16},{12,20},{16,24},{20,28},{24,32},{28,36},{32,40... | collective-permute-start | bytes 786440 | tf_op jit(solution)/shard_map/ppermute | solution.py:328
  78.8 19.6 %collective-permute-start.4 = (bf16[128,1024]{1,0:T(8,128)(2,1)S(1)}, bf16[128,1024]{1,0:T(8,128)(2,1)S(1)}, u32[]{:S(2)}, u32[]{:S(2)}) collective-permute-start(bf16[128,1024]{1,0:T(8,128)(2,1)S(1)} %collective-permute-done.2.k2_ref), channel_id=1, source_target_pairs={{0,4},{4,0},{8,12},{12,8},{16,20},{20,16},{24,28},{28,24},{32,36},... | collective-permute-start | bytes 786440 | tf_op jit(solution)/shard_map/ppermute | solution.py:332
  84.8 13.6 %collective-permute-start.3 = (bf16[128,1024]{1,0:T(8,128)(2,1)S(1)}, bf16[128,1024]{1,0:T(8,128)(2,1)S(1)}, u32[]{:S(2)}, u32[]{:S(2)}) collective-permute-start(bf16[128,1024]{1,0:T(8,128)(2,1)S(1)} %collective-permute-done.1.k1_ref), channel_id=1, source_target_pairs={{0,4},{4,0},{8,12},{12,8},{16,20},{20,16},{24,28},{28,24},{32,36},... | collective-permute-start | bytes 786440 | tf_op jit(solution)/shard_map/ppermute | solution.py:332
  87.1 19.1 %collective-permute-start.10 = (bf16[128,1024]{1,0:T(8,128)(2,1)}, bf16[128,1024]{1,0:T(8,128)(2,1)S(1)}, u32[]{:S(2)}, u32[]{:S(2)}) collective-permute-start(bf16[128,1024]{1,0:T(8,128)(2,1)} %shard_map.144.v0_ref), channel_id=1, source_target_pairs={{0,4},{4,24},{8,12},{12,32},{16,20},{20,40},{24,28},{28,48},{32,36... | collective-permute-start | bytes 786440 | tf_op jit(solution)/shard_map/ppermute | solution.py:336
  89.7 16.5 %collective-permute-start.9 = (bf16[128,1024]{1,0:T(8,128)(2,1)S(1)}, bf16[128,1024]{1,0:T(8,128)(2,1)S(1)}, u32[]{:S(2)}, u32[]{:S(2)}) collective-permute-start(bf16[128,1024]{1,0:T(8,128)(2,1)S(1)} %collective-permute-done.7.v2_ref), channel_id=1, source_target_pairs={{0,4},{4,0},{8,12},{12,8},{16,20},{20,16},{24,28},{28,24},{32,36},... | collective-permute-start | bytes 786440 | tf_op jit(solution)/shard_map/ppermute | solution.py:332
  95.7 10.4 %collective-permute-start.8 = (bf16[128,1024]{1,0:T(8,128)(2,1)S(1)}, bf16[128,1024]{1,0:T(8,128)(2,1)S(1)}, u32[]{:S(2)}, u32[]{:S(2)}) collective-permute-start(bf16[128,1024]{1,0:T(8,128)(2,1)S(1)} %collective-permute-done.6.v1_ref), channel_id=1, source_target_pairs={{0,4},{4,0},{8,12},{12,8},{16,20},{20,16},{24,28},{28,24},{32,36},... | collective-permute-start | bytes 786440 | tf_op jit(solution)/shard_map/ppermute | solution.py:332
  106.2 10.7 %copy-start.10 = (f32[1024]{0:T(1024)S(1)}, f32[1024]{0:T(1024)}, u32[]{:S(2)}) copy-start(f32[1024]{0:T(1024)} %param.23) | copy-start | bytes 12292

commit v2 on v1

--- a/solution.py
+++ b/solution.py
@@ -16,6 +16,8 @@
 ROWS = WIDTH // LANES
 NX, NZ, NQ = 4, 8, 4
 N_CTX = NX * NZ * NQ
+EVEN_STEPS = (0, 2, 4, 1, 3, 5)
+ODD_STEPS = (0, 2, 4, 3, 5, 1)
 
 orig_window = 8192.0
 rope_base = 10000.0
@@ -25,9 +27,11 @@
 bf16 = jnp.bfloat16
 
 
-def call(kernel, out_shape, args, scratch=(), smem=(), flops=1000000):
+def call(kernel, out_shape, args, scratch=(), smem=(), hbm=(), vmem=24, flops=1000000):
     specs = [
-        pl.BlockSpec(memory_space=pltpu.SMEM if i in smem else pltpu.VMEM)
+        pl.BlockSpec(
+            memory_space=pltpu.SMEM if i in smem else pltpu.HBM if i in hbm else pltpu.VMEM
+        )
         for i in range(len(args))
     ]
     single = not isinstance(out_shape, (list, tuple))
@@ -38,7 +42,7 @@
         in_specs=specs,
         out_specs=outs if single else [outs] * len(out_shape),
         scratch_shapes=list(scratch),
-        compiler_params=pltpu.CompilerParams(vmem_limit_bytes=24 * 1024 * 1024),
+        compiler_params=pltpu.CompilerParams(vmem_limit_bytes=vmem * 1024 * 1024),
         cost_estimate=pl.CostEstimate(flops=flops, bytes_accessed=1000000, transcendentals=0),
     )(*args)
 
@@ -77,7 +81,18 @@
     return [ref[m * ROWS : (m + 1) * ROWS, :] for m in range(MODES)]
 
 
-def rotate_kernel(q_ref, k_ref, cos_ref, sin_ref, qo_ref, ko_ref):
+def fetch(pairs, sems):
+    copies = [
+        pltpu.make_async_copy(src, dst, sems.at[i]) for i, (src, dst) in enumerate(pairs)
+    ]
+    for copy in copies:
+        copy.start()
+    return copies
+
+
+def rotate_kernel(q_hbm, k_hbm, cos_ref, sin_ref, qo_ref, ko_ref, q_ref, k_ref, sems):
+    for copy in fetch([(q_hbm, q_ref), (k_hbm, k_ref)], sems):
+        copy.wait()
     cosine = cos_ref[...]
     sine = sin_ref[...]
     for src, dst in ((k_ref, ko_ref), (q_ref, qo_ref)):
@@ -86,22 +101,35 @@
             dst[:, lane_block(h)] = (x * cosine + pltpu.roll(x, HEAD_DIM // 2, 1) * sine).astype(bf16)
 
 
-def local_kernel(
-    q_ref, k_ref, v_ref, taps_ref, res_ref, rate_ref,
-    l_ref, fq_ref, f0_ref, rr_ref, gg_ref, tp_ref, edge_ref,
-    qs, ks, vs, rs,
-):
+T_STATE, T_RATE, T_GAIN, T_TAP, T_EDGE, T_END = 0, 128, 256, 384, 456, 504
+
+
+def copy_kernel(src_ref, dst_ref):
+    dst_ref[...] = src_ref[...]
+
+
+def pair_kernel(a_ref, b_ref, out_ref):
+    out_ref[0] = a_ref[...]
+    out_ref[1] = b_ref[...]
+
+
+def local_kernel(h_ref, p_ref, l_ref, fq_ref, table_ref, qs, ks, vs, rs):
+    f0_ref = table_ref.at[T_STATE:T_RATE]
+    rr_ref = table_ref.at[T_RATE:T_GAIN]
+    gg_ref = table_ref.at[T_GAIN:T_TAP]
+    tp_ref = table_ref.at[T_TAP:T_EDGE]
+    edge_ref = table_ref.at[T_EDGE:T_END]
     for part in range(MODES // 8):
         for j in range(ROWS):
             rows = pl.ds(part * 8 * ROWS + j, 8, stride=ROWS)
-            rr_ref[rows, :] = rate_ref[part * 8 : part * 8 + 8, lane_block(j)]
-            rs[rows, :] = res_ref[part * 8 : part * 8 + 8, lane_block(j)]
-    for a in range(3):
-        for j in range(ROWS):
-            tp_ref[pl.ds(a * 3 * ROWS + j, 3, stride=ROWS), :] = taps_ref[a, :, lane_block(j)]
-    for src, dst in ((k_ref, ks), (v_ref, vs), (q_ref, qs)):
+            rr_ref[rows, :] = p_ref[part * 8 : part * 8 + 8, lane_block(j)]
+            rs[rows, :] = p_ref[MODES + part * 8 : MODES + part * 8 + 8, lane_block(j)]
+    for j in range(ROWS):
+        tp_ref[pl.ds(j, 8, stride=ROWS), :] = p_ref[2 * MODES : 2 * MODES + 8, lane_block(j)]
+        tp_ref[8 * ROWS + j : 8 * ROWS + j + 1, :] = p_ref[2 * MODES + 8 : 2 * MODES + 9, lane_block(j)]
+    for i, dst in enumerate((ks, vs, qs)):
         for g in range(TOK // 16):
-            block = src[g * 16 : (g + 1) * 16, :].astype(f32)
+            block = h_ref[i * TOK + g * 16 : i * TOK + (g + 1) * 16, :].astype(f32)
             for s in range(2):
                 for j in range(ROWS):
                     dst[pl.ds((g * 16 + s * 8) * ROWS + j, 8, stride=ROWS), :] = block[
@@ -139,10 +167,16 @@
         f0_ref[m * ROWS : (m + 1) * ROWS, :] = state[m]
 
 
-def edge_kernel(halo_ref, edge_ref, tp_ref, rr_ref, gg_ref, f0_ref, f_ref, em_ref, hs):
+def edge_kernel(halo_ref, table_ref, f_ref, em_ref, hs):
+    f0_ref = table_ref.at[T_STATE:T_RATE]
+    rr_ref = table_ref.at[T_RATE:T_GAIN]
+    gg_ref = table_ref.at[T_GAIN:T_TAP]
+    tp_ref = table_ref.at[T_TAP:T_EDGE]
+    edge_ref = table_ref.at[T_EDGE:T_END]
     halo = halo_ref[...].astype(f32)
-    for j in range(ROWS):
-        hs[pl.ds(j, 8, stride=ROWS), :] = halo[:, lane_block(j)]
+    for i in range(3):
+        for j in range(ROWS):
+            hs[pl.ds(i * 8 * ROWS + j, 8, stride=ROWS), :] = halo[i * 8 : i * 8 + 8, lane_block(j)]
 
     def row(ref, i):
         return ref[i * ROWS : (i + 1) * ROWS, :]
@@ -150,7 +184,7 @@
     tap = [row(tp_ref, i) for i in range(9)]
 
     def feats(i, base):
-        prev2, prev1 = row(hs, 2 * i), row(hs, 2 * i + 1)
+        prev2, prev1 = row(hs, 8 * i + 6), row(hs, 8 * i + 7)
         tok0, tok1 = row(edge_ref, 2 * i), row(edge_ref, 2 * i + 1)
         w = tap[base : base + 3]
         return (
@@ -172,46 +206,28 @@
                 row(f0_ref, m)
                 + gain * (jnp.exp(rate * -127.0) * m0 + jnp.exp(rate * -126.0) * m1)
             )
-        f_ref[i * 2 * ROWS : (i + 1) * 2 * ROWS, :] = jnp.concatenate(both, axis=0).astype(bf16)
-
-
-def weight(rate, span, steps):
-    factor = jnp.exp(rate * (jnp.maximum(steps, 0) * -span).astype(f32))
-    return jnp.where(steps >= 0, factor, 0.0)
-
-
-def quad_kernel(idx_ref, fq_ref, rr_ref, t_ref, before_ref):
-    q = idx_ref[2]
-    rate = rr_ref[...]
-    f = [fq_ref[i * LANES : (i + 1) * LANES, :].astype(f32) for i in range(NQ)]
-    d1 = jnp.exp(rate * -float(TOK))
-    total = f[0]
-    for i in range(1, NQ):
-        total = d1 * total + f[i]
-    total = total.astype(bf16)
-    for i in range(NZ):
-        t_ref[i] = total
-    before_ref[...] = tree_sum([weight(rate, TOK, q - 1 - i) * f[i] for i in range(NQ - 1)])
-
-
-def z_kernel(idx_ref, tz_ref, rr_ref, u_ref, before_ref):
+        both = jnp.concatenate(both, axis=0).astype(bf16)
+        for copy in range(NZ):
+            f_ref[copy, i * 2 * ROWS : (i + 1) * 2 * ROWS, :] = both
+
+
+def z_kernel(idx_ref, fz_ref, table_ref, u_ref, before_ref):
     z = idx_ref[1]
-    rate = rr_ref[...]
-    d = jnp.exp(rate * -float(TOK * NQ))
-    total = tz_ref[0].astype(f32)
+    d = jnp.exp(table_ref[T_RATE:T_GAIN, :] * -float(TOK * NQ))
+    total = fz_ref[0].astype(f32)
     before = jnp.zeros_like(total)
     for i in range(1, NZ):
         before = jnp.where(z == i, total, before)
-        total = d * total + tz_ref[i].astype(f32)
+        total = d * total + fz_ref[i].astype(f32)
     total = total.astype(bf16)
     for i in range(NX):
         u_ref[i] = total
     before_ref[...] = before
 
 
-def out_kernel(idx_ref, ux_ref, zb_ref, qb_ref, rr_ref, gg_ref, em_ref, l_ref, fq_ref, out_ref, cs, ys):
+def x_kernel(idx_ref, ux_ref, before_ref, f_ref, table_ref, y_ref):
     x, z, q = idx_ref[0], idx_ref[1], idx_ref[2]
-    rate = rr_ref[...]
+    rate = table_ref[T_RATE:T_GAIN, :]
     d = jnp.exp(rate * -float(TOK * NQ * NZ))
     carry = jnp.zeros_like(rate)
     running = ux_ref[0].astype(f32)
@@ -219,10 +235,24 @@
         carry = jnp.where(x == i, running, carry)
         if i < NX - 1:
             running = d * running + ux_ref[i].astype(f32)
-    group = zb_ref[...] + jnp.exp(rate * (z * -(TOK * NQ)).astype(f32)) * carry
-    own = qb_ref[...] + jnp.exp(rate * (q * -TOK).astype(f32)) * group
+    before = before_ref[...] + jnp.exp(rate * (z * -(TOK * NQ)).astype(f32)) * carry
+    after = jnp.exp(rate * -float(TOK * NQ)) * before + f_ref[0].astype(f32)
+    before, after = before.astype(bf16), after.astype(bf16)
+    for i in range(NQ):
+        y_ref[i] = jnp.where(q < i, after, before)
+
+
+def out_kernel(idx_ref, yq_ref, table_ref, em_ref, l_ref, fq_ref, out_ref, cs, ys):
+    q = idx_ref[2]
+    rate = table_ref[T_RATE:T_GAIN, :]
+    own = tree_sum(
+        [
+            jnp.exp(rate * (((q + 3 - i) % NQ) * -TOK).astype(f32)) * yq_ref[i].astype(f32)
+            for i in range(NQ)
+        ]
+    )
     decay_all = jnp.exp(-rate)
-    gain_all = gg_ref[...]
+    gain_all = table_ref[T_GAIN:T_TAP, :]
 
     def tile(value, m):
         return value[m * ROWS : (m + 1) * ROWS, :]
@@ -254,10 +284,11 @@
             out_ref[g * 16 : (g + 1) * 16, lane_block(j)] = jnp.concatenate(halves, axis=0).astype(bf16)
 
 
-def weights_kernel(mask_ref, q_ref, k0_ref, k1_ref, k2_ref, k3_ref, k4_ref, k5_ref, w_ref, inv_ref):
+def weights_kernel(idx_ref, mask_ref, q_ref, k0_ref, k1_ref, k2_ref, swap_ref, k5_ref, w_ref, inv_ref):
     yarn_scale = 0.1 * math.log(yarn_factor) + 1.0
     coef = yarn_scale * yarn_scale / math.sqrt(HEAD_DIM) * math.log2(math.e)
-    pieces = (k0_ref, k1_ref, k2_ref, k3_ref, k4_ref, k5_ref)
+    pieces = (k0_ref, k1_ref, k2_ref, swap_ref.at[0], swap_ref.at[1], k5_ref)
+    odd = idx_ref[2] % 2 == 1
     shape = (TOK, TOK)
     causal = lax.broadcasted_iota(jnp.int32, shape, 1) <= lax.broadcasted_iota(jnp.int32, shape, 0)
     lane = lax.broadcasted_iota(jnp.int32, (TOK, LANES), 1)
@@ -269,7 +300,7 @@
             s = lax.dot_general(
                 query, piece[:, lane_block(h)], (((1,), (1,)), ((), ())), preferred_element_type=f32
             ) * coef
-            allowed = mask_ref[i] == 1
+            allowed = mask_ref[0, jnp.where(odd, ODD_STEPS[i], EVEN_STEPS[i])] == 1
             visible = (causal & allowed) if i == 0 else jnp.broadcast_to(allowed, shape)
             scores.append(jnp.where(visible, s, -1e30))
         top = scores[0]
@@ -286,8 +317,8 @@
     inv_ref[...] = inverse
 
 
-def attend_kernel(w_ref, inv_ref, v0_ref, v1_ref, v2_ref, v3_ref, v4_ref, v5_ref, a_ref, sq_ref):
-    pieces = (v0_ref, v1_ref, v2_ref, v3_ref, v4_ref, v5_ref)
+def attend_kernel(w_ref, inv_ref, v0_ref, v1_ref, v2_ref, swap_ref, v5_ref, a_ref, sq_ref):
+    pieces = (v0_ref, v1_ref, v2_ref, swap_ref.at[0], swap_ref.at[1], v5_ref)
     inverse = inv_ref[...]
     squares = None
     for h in range(HEADS):
@@ -332,13 +363,18 @@
     return lax.ppermute(value, "ctx", [(i, i ^ 1) for i in range(N_CTX)])
 
 
-def window(value):
-    extra = lax.ppermute(
+def ahead_extra(value):
+    return lax.ppermute(
         value, "ctx", [(i, (i + (5 if i % 2 else 1)) % N_CTX) for i in range(N_CTX)]
     )
-    two = ahead(value, 2)
-    four = ahead(value, 4)
-    return [value, two, four, core_swap(two), core_swap(four), extra]
+
+
+def window_far(value):
+    return ahead(value, 2), ahead(value, 4), ahead_extra(value)
+
+
+def pair_of(a, b):
+    return call(pair_kernel, sds((2, TOK, WIDTH), bf16), (a, b))
 
 
 def local(
@@ -346,9 +382,9 @@
 ):
     me = lax.axis_index("ctx")
     idx = jnp.stack([me // (NZ * NQ), (me // NQ) % NZ, me % NQ]).astype(jnp.int32)
-    rim = jnp.concatenate(
-        [hyena_k[TOK - 2 :], hyena_v[TOK - 2 :], hyena_q[TOK - 2 :], hyena_q[TOK - 2 :]], axis=0
-    )
+    dma = pltpu.SemaphoreType.DMA
+    hyena = jnp.concatenate([hyena_k, hyena_v, hyena_q], axis=0)
+    rim = jnp.concatenate([hyena[(i + 1) * TOK - 8 : (i + 1) * TOK] for i in range(3)], axis=0)
     halo = lax.ppermute(rim, "ctx", [(i, i + 1) for i in range(N_CTX - 1)])
 
     angles = (offsets[me] + jnp.arange(TOK, dtype=jnp.int32)).astype(f32)[:, None] * head_freqs(HEAD_DIM)[None, :]
@@ -362,53 +398,61 @@
             jnp.concatenate([cosine, cosine], axis=1),
             jnp.concatenate([-sine, sine], axis=1),
         ),
-    )
-    key_pieces = window(k_rot)
+        scratch=[pltpu.VMEM((TOK, WIDTH), bf16)] * 2 + [dma((2,))],
+        hbm=(0, 1),
+    )
 
     big, small = sds((TOK * ROWS, LANES), f32), sds((MODES * ROWS, LANES), f32)
-    l_rest, feat_q, f0, rr, gg, tp, edge = call(
+    params = jnp.concatenate([rates, residues, short_taps.reshape(9, WIDTH)], axis=0)
+    l_rest, feat_q, table = call(
         local_kernel,
-        [big, big, small, small, small, sds((9 * ROWS, LANES), f32), sds((6 * ROWS, LANES), f32)],
-        (hyena_q, hyena_k, hyena_v, short_taps, residues, rates),
+        [big, big, sds((T_END, LANES), f32)],
+        (hyena, params),
         scratch=[pltpu.VMEM((TOK * ROWS, LANES), f32)] * 3 + [pltpu.VMEM((MODES * ROWS, LANES), f32)],
     )
     state, em = call(
         edge_kernel,
-        [sds((MODES * ROWS, LANES), bf16), sds((4 * ROWS, LANES), f32)],
-        (halo, edge, tp, rr, gg, f0),
-        scratch=[pltpu.VMEM((8 * ROWS, LANES), f32)],
-    )
-    quad = lax.all_gather(state, "ctx", axis_index_groups=quad_groups(), tiled=True)
-    group, quad_before = call(
-        quad_kernel, [sds((NZ, MODES * ROWS, LANES), bf16), small], (idx, quad, rr), smem=(0,)
-    )
-    along_z = lax.all_to_all(group, "ctx", 0, 0, tiled=True, axis_index_groups=z_groups())
-    column, z_before = call(
-        z_kernel, [sds((NX, MODES * ROWS, LANES), bf16), small], (idx, along_z, rr), smem=(0,)
-    )
+        [sds((NZ, MODES * ROWS, LANES), bf16), sds((4 * ROWS, LANES), f32)],
+        (halo, table),
+        scratch=[pltpu.VMEM((24 * ROWS, LANES), f32)],
+    )
+    along_z = lax.all_to_all(state, "ctx", 0, 0, tiled=True, axis_index_groups=z_groups())
+    column, before = call(
+        z_kernel, [sds((NX, MODES * ROWS, LANES), bf16), small], (idx, along_z, table), smem=(0,)
+    )
+    k_two = ahead(k_rot, 2)
+    column, k_late = lax.optimization_barrier((column, k_rot))
+    k_extra = ahead_extra(call(copy_kernel, sds((TOK, WIDTH), bf16), (k_late,), flops=5_000_000_000))
     along_x = lax.all_to_all(column, "ctx", 0, 0, tiled=True, axis_index_groups=x_groups())
+    classes = call(
+        x_kernel, sds((NQ, MODES * ROWS, LANES), bf16), (idx, along_x, before, state, table), smem=(0,)
+    )
+    classes, k_late = lax.optimization_barrier((classes, k_late))
+    k_four = ahead(call(copy_kernel, sds((TOK, WIDTH), bf16), (k_late,), flops=5_000_000_000), 4)
+    quad = lax.all_to_all(classes, "ctx", 0, 0, tiled=True, axis_index_groups=quad_groups())
+    quad, k_extra, k_two = lax.optimization_barrier((quad, k_extra, k_two))
     hyena_out = call(
         out_kernel,
         sds((TOK, WIDTH), bf16),
-        (idx, along_x, z_before, quad_before, rr, gg, em, l_rest, feat_q),
+        (idx, quad, table, em, l_rest, feat_q),
         scratch=[pltpu.VMEM((MODES * ROWS, LANES), f32), pltpu.VMEM((TOK * ROWS, LANES), f32)],
         smem=(0,),
     )
-    value_pieces = window(hyena_out)
-
-    order = jnp.where(
-        me % 2 == 0, jnp.array([0, 2, 4, 1, 3, 5], jnp.int32), jnp.array([0, 2, 4, 3, 5, 1], jnp.int32)
-    )
+    v_two, v_four, v_extra = window_far(hyena_out)
+    k_two, hyena_late = lax.optimization_barrier((k_two, hyena_out))
+    k_swap = core_swap(pair_of(k_two, k_four))
+    v_two, v_extra = lax.optimization_barrier((v_two, v_extra))
+    v_swap = core_swap(pair_of(v_two, v_four))
     weights, inverse = call(
         weights_kernel,
         [sds((HEADS, TOK, 6 * TOK), bf16), sds((TOK, LANES), f32)],
-        (block_mask[0][order], q_rot, *key_pieces),
-        smem=(0,),
+        (idx, block_mask, q_rot, k_rot, k_two, k_four, k_swap, k_extra),
+        smem=(0, 1),
     )
     attended, squares = call(
         attend_kernel,
         [sds((TOK, WIDTH), f32), sds((1, TOK), f32)],
-        (weights, inverse, *value_pieces),
+        (weights, inverse, hyena_out, v_two, v_four, v_swap, v_extra),
     )
     total = lax.psum(squares, "ch")
     attn_out = call(norm_kernel, sds((TOK, WIDTH), bf16), (attended, total, out_gain[None, :]))

time: 120 us -> 114 us (0.950)
  waiting for transfers between devices: 30.2 us -> 38.8 us
  blocking collectives: 19.3 us -> 11.5 us
  local copies, waits for them, and re-layouts: 8.78 us -> 2.86 us
  starting transfers between devices: 46.6 us -> 43.1 us
  Pallas kernels: 10.6 us -> 12.6 us
    all_gather x1 -> x0, blocking collectives: 9.33 us -> none  [local(): lax.all_gather(state, 'ctx', axis_index_groups=quad_groups(), tiled=True)]
    unnamed x28 -> x18, local copies, waits for them, and re-layouts: 5.36 us -> 0.05 us
    ppermute x2, waiting for transfers between devices: 5.46 us -> 10.6 us  [ahead_extra(): lax.ppermute(value, 'ctx', [(i, (i + (5 if i % 2 else 1)) % N_CTX) for i...]
    ppermute x4 -> x2, starting transfers between devices: 14.5 us -> 10.6 us  [core_swap(): return lax.ppermute(value, 'ctx', [(i, i ^ 1) for i in range(N_CTX)])]
    ppermute x1, waiting for transfers between devices: 8.1 us -> 11.3 us  [local(): halo = lax.ppermute(rim, 'ctx', [(i, i + 1) for i in range(N_CTX - 1)])]
    all_to_all x1 -> x2, waiting for transfers between devices: 10.6 us -> 7.64 us  [the longest x1 6.71 us: local(): lax.all_to_all(state, 'ctx', 0, 0, tiled=True, axis_index_groups=z_groups())]
    all_to_all x1 -> x2, starting transfers between devices: 6.85 us -> 9.03 us  [the longest x1 4.97 us: local(): lax.all_to_all(classes, 'ctx', 0, 0, tiled=True, axis_index_groups=quad_g...]
    pallas_call x9 -> x13, Pallas kernels: 10.6 us -> 12.6 us  [call(): pl.pallas_call(kernel, out_shape=out_shape, in_specs=specs, out_specs=out...]
  transfers between devices with their start and end apart: 13 -> 12, of which waited for: 6 -> 7; matrix products, arithmetic and copies ran while one was open for 2% -> 3% of each run, Pallas kernels for 6% -> 9%
where the time goes in v2:
time: 114 us; the launch traced here: 112 us
  starting transfers between devices  43.1 us (38%)
  waiting for transfers between devices  38.8 us (34%)
  Pallas kernels  12.6 us (11%)
  blocking collectives  11.5 us (10%)
  local copies, waits for them, and re-layouts  2.86 us (3%)
  other arithmetic  2.34 us (2%)
    ppermute x4, starting transfers between devices, ahead(): lax.ppermute(value, 'ctx', [(i, (i + steps) % N_CTX) for i in range(N_CTX)])  13.1 us
    pallas_call x13, Pallas kernels, call(): pl.pallas_call(kernel, out_shape=out_shape, in_specs=specs, out_specs=out...  12.6 us
    psum x1, blocking collectives, local(): total = lax.psum(squares, 'ch')  11.5 us
    ppermute x1, waiting for transfers between devices, local(): halo = lax.ppermute(rim, 'ctx', [(i, i + 1) for i in range(N_CTX - 1)])  11.3 us
    ppermute x2, waiting for transfers between devices, ahead_extra(): lax.ppermute(value, 'ctx', [(i, (i + (5 if i % 2 else 1)) % N_CTX) for i...  10.6 us
    ppermute x2, starting transfers between devices, core_swap(): return lax.ppermute(value, 'ctx', [(i, i ^ 1) for i in range(N_CTX)])  10.6 us
    ppermute x4, waiting for transfers between devices, ahead(): lax.ppermute(value, 'ctx', [(i, (i + steps) % N_CTX) for i in range(N_CTX)])  7.98 us
    all_to_all x1, waiting for transfers between devices, local(): lax.all_to_all(state, 'ctx', 0, 0, tiled=True, axis_index_groups=z_groups())  6.71 us
  transfers between devices with their start and end apart: 12, of which 7 were waited for; matrix products, arithmetic and copies ran while one was open for 3% of the time, Pallas kernels for 9%

profile of v2, /device:TPU:6, one launch (start us, length us, event | category | flops | bytes accessed | tf_op | source)
XLA Modules:
  0.0 112.3 jit_solution(12232907422013372821)
XLA Ops:
  0.7 0.8 slice.11
  1.4 0.7 slice.10
  2.2 0.7 slice.9
  2.9 1.9 %collective-permute-start = (bf16[24,1024]{1,0:T(8,128)(2,1)S(1)}, bf16[24,1024]{1,0:T(8,128)(2,1)S(1)}, u32[]{:S(2)}, u32[]{:S(2)}) collective-permute-start(bf16[24,1024]{1,0:T(8,128)(2,1)S(1)} %pad_maximum_fusion.4), channel_id=1, source_target_pairs={{0,4},{4,8},{8,12},{12,16},{16,20},{20,24},{24,28},{28,32},{32,36}... | collective-permute-start | bytes 147464 | tf_op jit(solution)/shard_map/ppermute | solution.py:388
  4.8 1.2 %pad_maximum_fusion.h_ref = bf16[384,1024]{1,0:T(8,128)(2,1)S(1)} fusion(bf16[128,1024]{1,0:T(8,128)(2,1)} %param.11, bf16[128,1024]{1,0:T(8,128)(2,1)} %param.13, bf16[128,1024]{1,0:T(8,128)(2,1)} %param.12), kind=kLoop, calls=%fused_computation | loop fusion | flops 2359296 | bytes 1572864 | tf_op jit(solution)/shard_map/concatenate | solution.py:386
  6.0 0.0 copy-start.1
  6.0 0.0 copy-start.2
  6.1 0.6 dynamic_slice.3
  6.7 0.7 add_convert_fusion
  7.3 1.9 %shard_map.122 = (f32[1024,128]{1,0:T(8,128)S(1)}, f32[1024,128]{1,0:T(8,128)S(1)}, f32[504,128]{1,0:T(8,128)S(1)}) custom-call(bf16[384,1024]{1,0:T(8,128)(2,1)S(1)} %pad_maximum_fusion.h_ref, f32[41,1024]{1,0:T(8,128)S(1)} %pad_maximum_fusion.1.p_ref), custom_call_target="tpu_custom_call" | custom-call | flops 1000000 | bytes 1000000 | tf_op jit(solution)/shard_map/pallas_call | solution.py:39
  9.2 11.3 %collective-permute-done.halo_ref = bf16[24,1024]{1,0:T(8,128)(2,1)S(1)} collective-permute-done((bf16[24,1024]{1,0:T(8,128)(2,1)S(1)}, bf16[24,1024]{1,0:T(8,128)(2,1)S(1)}, u32[]{:S(2)}, u32[]{:S(2)}) %collective-permute-start) | collective-permute-done | bytes 49184 | tf_op jit(solution)/shard_map/ppermute | solution.py:388
  20.6 0.8 shard_map.123
  21.3 4.1 %all-to-all-start = ((bf16[8,128,128]{2,1,0:T(8,128)(2,1)}), bf16[8,128,128]{2,1,0:T(8,128)(2,1)S(1)}, u32[]{:S(2)}, u32[]{:S(2)}) async-start(bf16[8,128,128]{2,1,0:T(8,128)(2,1)} %get-tuple-element.26.f_ref), calls=%async_computation | async-start | bytes 524288 | tf_op jit(solution)/shard_map/all_to_all | solution.py:419
  25.4 0.3 fusion
  25.7 0.1 pad_maximum_fusion.2
  25.8 0.3 shard_map.125
  26.2 5.6 %collective-permute-start.2 = (bf16[128,1024]{1,0:T(8,128)(2,1)S(1)}, bf16[128,1024]{1,0:T(8,128)(2,1)S(1)}, u32[]{:S(2)}, u32[]{:S(2)}) collective-permute-start(bf16[128,1024]{1,0:T(8,128)(2,1)S(1)} %get-tuple-element.40.src_ref.k0_ref), channel_id=1, source_target_pairs={{0,8},{4,12},{8,16},{12,20},{16,24},{20,28},{24,32},{28,36},{32,40... | collective-permute-start | bytes 786440 | tf_op jit(solution)/shard_map/ppermute | solution.py:359
  31.8 0.1 pad_add_fusion.idx_ref
  31.9 6.7 %all-to-all-done.fz_ref = bf16[8,128,128]{2,1,0:T(8,128)(2,1)S(1)} async-done(((bf16[8,128,128]{2,1,0:T(8,128)(2,1)}), bf16[8,128,128]{2,1,0:T(8,128)(2,1)S(1)}, u32[]{:S(2)}, u32[]{:S(2)}) %all-to-all-start) | async-done | bytes 262176 | tf_op jit(solution)/shard_map/all_to_all | solution.py:419
  38.6 1.3 %shard_map.124 = (bf16[4,128,128]{2,1,0:T(8,128)(2,1)}, f32[128,128]{1,0:T(8,128)S(1)}) custom-call(s32[3]{0:T(128)S(1)} %pad_add_fusion.idx_ref, bf16[8,128,128]{2,1,0:T(8,128)(2,1)S(1)} %all-to-all-done.fz_ref, f32[504,128]{1,0:T(8,128)S(1)} %get-tuple-element.25.table_ref), custom_call_target="tpu_custom_call" | custom-call | flops 1000000 | bytes 1000000 | tf_op jit(solution)/shard_map/pallas_call | solution.py:39
  39.9 4.7 %all-to-all-start.1 = ((bf16[4,128,128]{2,1,0:T(8,128)(2,1)}), bf16[4,128,128]{2,1,0:T(8,128)(2,1)S(1)}, u32[]{:S(2)}, u32[]{:S(2)}) async-start(bf16[4,128,128]{2,1,0:T(8,128)(2,1)} %get-tuple-element.29), calls=%async_computation.1 | async-start | bytes 262144 | tf_op jit(solution)/shard_map/all_to_all | solution.py:426
  44.6 0.7 shard_map.127
  45.3 1.9 %collective-permute-start.1 = (bf16[128,1024]{1,0:T(8,128)(2,1)}, bf16[128,1024]{1,0:T(8,128)(2,1)S(1)}, u32[]{:S(2)}, u32[]{:S(2)}) collective-permute-start(bf16[128,1024]{1,0:T(8,128)(2,1)} %shard_map.127), channel_id=1, source_target_pairs={{0,4},{4,24},{8,12},{12,32},{16,20},{20,40},{24,28},{28,48},{32,36... | collective-permute-start | bytes 786440 | tf_op jit(solution)/shard_map/ppermute | solution.py:367
  47.2 1.3 %all-to-all-done.1.ux_ref = bf16[4,128,128]{2,1,0:T(8,128)(2,1)S(1)} async-done(((bf16[4,128,128]{2,1,0:T(8,128)(2,1)}), bf16[4,128,128]{2,1,0:T(8,128)(2,1)S(1)}, u32[]{:S(2)}, u32[]{:S(2)}) %all-to-all-start.1) | async-done | bytes 131104 | tf_op jit(solution)/shard_map/all_to_all | solution.py:426
  48.5 1.7 %shard_map.126 = bf16[4,128,128]{2,1,0:T(8,128)(2,1)} custom-call(s32[3]{0:T(128)S(1)} %pad_add_fusion.idx_ref, bf16[4,128,128]{2,1,0:T(8,128)(2,1)S(1)} %all-to-all-done.1.ux_ref, f32[128,128]{1,0:T(8,128)S(1)} %get-tuple-element.30.before_ref, bf16[8,128,128]{2,1,0:T(8,128)(2,1)} %get-tuple-element.26.f_ref, f32[504,128]{1,0:T(8,128)S(1)} %get-tuple-element.25.table_ref), custom_call_target="tpu_custom_call" | custom-call | flops 1000000 | bytes 1000000 | tf_op jit(solution)/shard_map/pallas_call | solution.py:39
  50.2 5.0 %all-to-all-start.2 = ((bf16[4,128,128]{2,1,0:T(8,128)(2,1)}), bf16[4,128,128]{2,1,0:T(8,128)(2,1)S(1)}, u32[]{:S(2)}, u32[]{:S(2)}) async-start(bf16[4,128,128]{2,1,0:T(8,128)(2,1)} %shard_map.126), calls=%async_computation.2 | async-start | bytes 262144 | tf_op jit(solution)/shard_map/all_to_all | solution.py:432
  55.2 2.4 %collective-permute-start.3 = (bf16[128,1024]{1,0:T(8,128)(2,1)S(1)}, bf16[128,1024]{1,0:T(8,128)(2,1)S(1)}, u32[]{:S(2)}, u32[]{:S(2)}) collective-permute-start(bf16[128,1024]{1,0:T(8,128)(2,1)S(1)} %shard_map.129), channel_id=1, source_target_pairs={{0,16},{4,20},{8,24},{12,28},{16,32},{20,36},{24,40},{28,44},{32,4... | collective-permute-start | bytes 786440 | tf_op jit(solution)/shard_map/ppermute | solution.py:359
  57.6 0.0 collective-permute-done.2.a_ref.k1_ref
  57.6 5.2 %collective-permute-done.1.k5_ref = bf16[128,1024]{1,0:T(8,128)(2,1)S(1)} collective-permute-done((bf16[128,1024]{1,0:T(8,128)(2,1)}, bf16[128,1024]{1,0:T(8,128)(2,1)S(1)}, u32[]{:S(2)}, u32[]{:S(2)}) %collective-permute-start.1) | collective-permute-done | bytes 262176 | tf_op jit(solution)/shard_map/ppermute | solution.py:367
  62.9 0.9 all-to-all-done.2.yq_ref
  63.8 2.1 %shard_map.128.v0_ref = bf16[128,1024]{1,0:T(8,128)(2,1)} custom-call(s32[3]{0:T(128)S(1)} %pad_add_fusion.idx_ref, bf16[4,128,128]{2,1,0:T(8,128)(2,1)S(1)} %all-to-all-done.2.yq_ref, f32[504,128]{1,0:T(8,128)S(1)} %get-tuple-element.25.table_ref, f32[32,128]{1,0:T(8,128)S(1)} %get-tuple-element.34.em_ref, f32[1024,128]{1,0:T(8,128)S(1)} %get-tuple-element.35.l_ref, ...), custom_call_target="tpu_custom_call" | custom-call | flops 1000000 | bytes 1000000 | tf_op jit(solution)/shard_map/pallas_call | solution.py:39
  65.9 2.8 %collective-permute-start.5 = (bf16[128,1024]{1,0:T(8,128)(2,1)}, bf16[128,1024]{1,0:T(8,128)(2,1)S(1)}, u32[]{:S(2)}, u32[]{:S(2)}) collective-permute-start(bf16[128,1024]{1,0:T(8,128)(2,1)} %shard_map.128.v0_ref), channel_id=1, source_target_pairs={{0,8},{4,12},{8,16},{12,20},{16,24},{20,28},{24,32},{28,36},{32,40... | collective-permute-start | bytes 786440 | tf_op jit(solution)/shard_map/ppermute | solution.py:359
  68.7 1.9 %collective-permute-start.6 = (bf16[128,1024]{1,0:T(8,128)(2,1)}, bf16[128,1024]{1,0:T(8,128)(2,1)S(1)}, u32[]{:S(2)}, u32[]{:S(2)}) collective-permute-start(bf16[128,1024]{1,0:T(8,128)(2,1)} %shard_map.128.v0_ref), channel_id=1, source_target_pairs={{0,4},{4,24},{8,12},{12,32},{16,20},{20,40},{24,28},{28,48},{32,36... | collective-permute-start | bytes 786440 | tf_op jit(solution)/shard_map/ppermute | solution.py:367
  70.6 2.3 %collective-permute-start.7 = (bf16[128,1024]{1,0:T(8,128)(2,1)}, bf16[128,1024]{1,0:T(8,128)(2,1)S(1)}, u32[]{:S(2)}, u32[]{:S(2)}) collective-permute-start(bf16[128,1024]{1,0:T(8,128)(2,1)} %shard_map.128.v0_ref), channel_id=1, source_target_pairs={{0,16},{4,20},{8,24},{12,28},{16,32},{20,36},{24,40},{28,44},{32,4... | collective-permute-start | bytes 786440 | tf_op jit(solution)/shard_map/ppermute | solution.py:359
  72.9 0.0 collective-permute-done.3.b_ref.k2_ref
  73.0 0.0 copy-start
  73.0 8.3 %collective-permute-start.4 = (bf16[2,128,1024]{2,1,0:T(8,128)(2,1)S(1)}, bf16[2,128,1024]{2,1,0:T(8,128)(2,1)S(1)}, u32[]{:S(2)}, u32[]{:S(2)}) collective-permute-start(bf16[2,128,1024]{2,1,0:T(8,128)(2,1)S(1)} %shard_map.130), channel_id=1, source_target_pairs={{0,4},{4,0},{8,12},{12,8},{16,20},{20,16},{24,28},{28,24},{32,36},... | collective-permute-start | bytes 1572872 | tf_op jit(solution)/shard_map/ppermute | solution.py:363
  81.3 8.0 %collective-permute-done.5.a_ref.v1_ref = bf16[128,1024]{1,0:T(8,128)(2,1)S(1)} collective-permute-done((bf16[128,1024]{1,0:T(8,128)(2,1)}, bf16[128,1024]{1,0:T(8,128)(2,1)S(1)}, u32[]{:S(2)}, u32[]{:S(2)}) %collective-permute-start.5) | collective-permute-done | bytes 262176 | tf_op jit(solution)/shard_map/ppermute | solution.py:359
  89.2 5.3 %collective-permute-done.6.v5_ref = bf16[128,1024]{1,0:T(8,128)(2,1)S(1)} collective-permute-done((bf16[128,1024]{1,0:T(8,128)(2,1)}, bf16[128,1024]{1,0:T(8,128)(2,1)S(1)}, u32[]{:S(2)}, u32[]{:S(2)}) %collective-permute-start.6) | collective-permute-done | bytes 262176 | tf_op jit(solution)/shard_map/ppermute | solution.py:367
  94.6 0.0 collective-permute-done.7.b_ref.v2_ref
  94.6 2.3 %collective-permute-start.8 = (bf16[2,128,1024]{2,1,0:T(8,128)(2,1)S(1)}, bf16[2,128,1024]{2,1,0:T(8,128)(2,1)S(1)}, u32[]{:S(2)}, u32[]{:S(2)}) collective-permute-start(bf16[2,128,1024]{2,1,0:T(8,128)(2,1)S(1)} %shard_map.132), channel_id=1, source_target_pairs={{0,4},{4,0},{8,12},{12,8},{16,20},{20,16},{24,28},{28,24},{32,36},... | collective-permute-start | bytes 1572872 | tf_op jit(solution)/shard_map/ppermute | solution.py:363
  96.9 0.0 collective-permute-done.4.swap_ref
  96.9 2.3 %shard_map.131 = (bf16[8,128,768]{2,1,0:T(8,128)(2,1)S(1)}, f32[128,128]{1,0:T(8,128)S(1)}) custom-call(s32[3]{0:T(128)S(1)} %pad_add_fusion.idx_ref, s32[1,6]{1,0:T(1,128)S(1)} %copy-done.4, bf16[128,1024]{1,0:T(8,128)(2,1)S(1)} %get-tuple-element.37.q_ref, bf16[128,1024]{1,0:T(8,128)(2,1)S(1)} %get-tuple-element.40.src_ref.k0_ref, ...), custom_call_target="tpu_custom_call" | custom-call | flops 1000000 | bytes 1000000 | tf_op jit(solution)/shard_map/pallas_call | solution.py:39
  99.2 0.0 collective-permute-done.8.swap_ref
  99.2 0.0 copy-start.3
  99.2 0.7 shard_map.133
  99.9 11.5 %psum.7.sq_ref = f32[1,128]{1,0:T(1,128)S(1)} all-reduce(f32[1,128]{1,0:T(1,128)S(1)} %get-tuple-element.47), channel_id=1, replica_groups=mesh['ctx'=128,'ch'=4] {'ch'}, use_global_device_ids=true, to_apply=%region_0.1 | all-reduce | flops 128 | bytes 1024 | tf_op jit(solution)/shard_map/psum | solution.py:457
  111.4 0.8 shard_map.134
  (21 shorter events, 0.2 us)
Async XLA Ops:
  0.6 5.4 %copy-start.7 = (f32[3,3,1024]{2,1,0:T(4,128)S(1)}, f32[3,3,1024]{2,1,0:T(4,128)}, u32[]{:S(2)}) copy-start(f32[3,3,1024]{2,1,0:T(4,128)} %param.14) | copy-start | bytes 110596
  0.6 5.4 %copy-start.8 = (s32[128]{0:T(128)S(1)}, s32[128]{0:T(128)}, u32[]{:S(2)}) copy-start(s32[128]{0:T(128)} %param.19) | copy-start | bytes 1540
  0.7 6.0 %copy-start.5 = (f32[16,1024]{1,0:T(8,128)S(1)}, f32[16,1024]{1,0:T(8,128)}, u32[]{:S(2)}) copy-start(f32[16,1024]{1,0:T(8,128)} %param.15) | copy-start | bytes 196612
  0.7 6.0 %copy-start.6 = (f32[16,1024]{1,0:T(8,128)S(1)}, f32[16,1024]{1,0:T(8,128)}, u32[]{:S(2)}) copy-start(f32[16,1024]{1,0:T(8,128)} %param.16) | copy-start | bytes 196612
  2.9 17.7 %collective-permute-start = (bf16[24,1024]{1,0:T(8,128)(2,1)S(1)}, bf16[24,1024]{1,0:T(8,128)(2,1)S(1)}, u32[]{:S(2)}, u32[]{:S(2)}) collective-permute-start(bf16[24,1024]{1,0:T(8,128)(2,1)S(1)} %pad_maximum_fusion.4), channel_id=1, source_target_pairs={{0,4},{4,8},{8,12},{12,16},{16,20},{20,24},{24,28},{28,32},{32,36}... | collective-permute-start | bytes 147464 | tf_op jit(solution)/shard_map/ppermute | solution.py:388
  6.0 19.8 %copy-start.1 = (bf16[128,1024]{1,0:T(8,128)(2,1)S(1)}, bf16[128,1024]{1,0:T(8,128)(2,1)}, u32[]{:S(2)}) copy-start(bf16[128,1024]{1,0:T(8,128)(2,1)} %q_hbm.1) | copy-start | bytes 786436
  6.0 19.8 %copy-start.2 = (bf16[128,1024]{1,0:T(8,128)(2,1)S(1)}, bf16[128,1024]{1,0:T(8,128)(2,1)}, u32[]{:S(2)}) copy-start(bf16[128,1024]{1,0:T(8,128)(2,1)} %k_hbm.1) | copy-start | bytes 786436
  21.3 17.3 %all-to-all-start = ((bf16[8,128,128]{2,1,0:T(8,128)(2,1)}), bf16[8,128,128]{2,1,0:T(8,128)(2,1)S(1)}, u32[]{:S(2)}, u32[]{:S(2)}) async-start(bf16[8,128,128]{2,1,0:T(8,128)(2,1)} %get-tuple-element.26.f_ref), calls=%async_computation | async-start | bytes 524288 | tf_op jit(solution)/shard_map/all_to_all | solution.py:419
  26.2 31.5 %collective-permute-start.2 = (bf16[128,1024]{1,0:T(8,128)(2,1)S(1)}, bf16[128,1024]{1,0:T(8,128)(2,1)S(1)}, u32[]{:S(2)}, u32[]{:S(2)}) collective-permute-start(bf16[128,1024]{1,0:T(8,128)(2,1)S(1)} %get-tuple-element.40.src_ref.k0_ref), channel_id=1, source_target_pairs={{0,8},{4,12},{8,16},{12,20},{16,24},{20,28},{24,32},{28,36},{32,40... | collective-permute-start | bytes 786440 | tf_op jit(solution)/shard_map/ppermute | solution.py:359
  39.9 8.6 %all-to-all-start.1 = ((bf16[4,128,128]{2,1,0:T(8,128)(2,1)}), bf16[4,128,128]{2,1,0:T(8,128)(2,1)S(1)}, u32[]{:S(2)}, u32[]{:S(2)}) async-start(bf16[4,128,128]{2,1,0:T(8,128)(2,1)} %get-tuple-element.29), calls=%async_computation.1 | async-start | bytes 262144 | tf_op jit(solution)/shard_map/all_to_all | solution.py:426
  45.3 17.6 %collective-permute-start.1 = (bf16[128,1024]{1,0:T(8,128)(2,1)}, bf16[128,1024]{1,0:T(8,128)(2,1)S(1)}, u32[]{:S(2)}, u32[]{:S(2)}) collective-permute-start(bf16[128,1024]{1,0:T(8,128)(2,1)} %shard_map.127), channel_id=1, source_target_pairs={{0,4},{4,24},{8,12},{12,32},{16,20},{20,40},{24,28},{28,48},{32,36... | collective-permute-start | bytes 786440 | tf_op jit(solution)/shard_map/ppermute | solution.py:367
  50.2 13.6 %all-to-all-start.2 = ((bf16[4,128,128]{2,1,0:T(8,128)(2,1)}), bf16[4,128,128]{2,1,0:T(8,128)(2,1)S(1)}, u32[]{:S(2)}, u32[]{:S(2)}) async-start(bf16[4,128,128]{2,1,0:T(8,128)(2,1)} %shard_map.126), calls=%async_computation.2 | async-start | bytes 262144 | tf_op jit(solution)/shard_map/all_to_all | solution.py:432
  55.2 17.7 %collective-permute-start.3 = (bf16[128,1024]{1,0:T(8,128)(2,1)S(1)}, bf16[128,1024]{1,0:T(8,128)(2,1)S(1)}, u32[]{:S(2)}, u32[]{:S(2)}) collective-permute-start(bf16[128,1024]{1,0:T(8,128)(2,1)S(1)} %shard_map.129), channel_id=1, source_target_pairs={{0,16},{4,20},{8,24},{12,28},{16,32},{20,36},{24,40},{28,44},{32,4... | collective-permute-start | bytes 786440 | tf_op jit(solution)/shard_map/ppermute | solution.py:359
  63.8 33.1 %copy-start.4 = (s32[1,6]{1,0:T(1,128)S(1)}, s32[1,6]{1,0:T(1,128)}, u32[]{:S(2)}) copy-start(s32[1,6]{1,0:T(1,128)} %mask_ref.1) | copy-start | bytes 76
  65.9 23.4 %collective-permute-start.5 = (bf16[128,1024]{1,0:T(8,128)(2,1)}, bf16[128,1024]{1,0:T(8,128)(2,1)S(1)}, u32[]{:S(2)}, u32[]{:S(2)}) collective-permute-start(bf16[128,1024]{1,0:T(8,128)(2,1)} %shard_map.128.v0_ref), channel_id=1, source_target_pairs={{0,8},{4,12},{8,16},{12,20},{16,24},{20,28},{24,32},{28,36},{32,40... | collective-permute-start | bytes 786440 | tf_op jit(solution)/shard_map/ppermute | solution.py:359
  68.7 25.9 %collective-permute-start.6 = (bf16[128,1024]{1,0:T(8,128)(2,1)}, bf16[128,1024]{1,0:T(8,128)(2,1)S(1)}, u32[]{:S(2)}, u32[]{:S(2)}) collective-permute-start(bf16[128,1024]{1,0:T(8,128)(2,1)} %shard_map.128.v0_ref), channel_id=1, source_target_pairs={{0,4},{4,24},{8,12},{12,32},{16,20},{20,40},{24,28},{28,48},{32,36... | collective-permute-start | bytes 786440 | tf_op jit(solution)/shard_map/ppermute | solution.py:367
  70.6 24.0 %collective-permute-start.7 = (bf16[128,1024]{1,0:T(8,128)(2,1)}, bf16[128,1024]{1,0:T(8,128)(2,1)S(1)}, u32[]{:S(2)}, u32[]{:S(2)}) collective-permute-start(bf16[128,1024]{1,0:T(8,128)(2,1)} %shard_map.128.v0_ref), channel_id=1, source_target_pairs={{0,16},{4,20},{8,24},{12,28},{16,32},{20,36},{24,40},{28,44},{32,4... | collective-permute-start | bytes 786440 | tf_op jit(solution)/shard_map/ppermute | solution.py:359
  73.0 26.3 %copy-start = (bf16[128,1024]{1,0:T(8,128)(2,1)S(1)}, bf16[128,1024]{1,0:T(8,128)(2,1)}, u32[]{:S(2)}) copy-start(bf16[128,1024]{1,0:T(8,128)(2,1)} %shard_map.128.v0_ref) | copy-start | bytes 786436
  73.0 23.9 %collective-permute-start.4 = (bf16[2,128,1024]{2,1,0:T(8,128)(2,1)S(1)}, bf16[2,128,1024]{2,1,0:T(8,128)(2,1)S(1)}, u32[]{:S(2)}, u32[]{:S(2)}) collective-permute-start(bf16[2,128,1024]{2,1,0:T(8,128)(2,1)S(1)} %shard_map.130), channel_id=1, source_target_pairs={{0,4},{4,0},{8,12},{12,8},{16,20},{20,16},{24,28},{28,24},{32,36},... | collective-permute-start | bytes 1572872 | tf_op jit(solution)/shard_map/ppermute | solution.py:363
  94.6 4.6 %collective-permute-start.8 = (bf16[2,128,1024]{2,1,0:T(8,128)(2,1)S(1)}, bf16[2,128,1024]{2,1,0:T(8,128)(2,1)S(1)}, u32[]{:S(2)}, u32[]{:S(2)}) collective-permute-start(bf16[2,128,1024]{2,1,0:T(8,128)(2,1)S(1)} %shard_map.132), channel_id=1, source_target_pairs={{0,4},{4,0},{8,12},{12,8},{16,20},{20,16},{24,28},{28,24},{32,36},... | collective-permute-start | bytes 1572872 | tf_op jit(solution)/shard_map/ppermute | solution.py:363
  99.2 12.2 %copy-start.3 = (f32[1024]{0:T(1024)S(1)}, f32[1024]{0:T(1024)}, u32[]{:S(2)}) copy-start(f32[1024]{0:T(1024)} %param.21) | copy-start | bytes 12292

commit v3 on v2

--- a/solution.py
+++ b/solution.py
@@ -88,6 +88,19 @@
     for copy in copies:
         copy.start()
     return copies
+
+
+def rim_kernel(k_hbm, v_hbm, q_hbm, out_ref, ks, vs, qs, sems):
+    last = pl.ds(TOK - 16, 16)
+    for copy in fetch(
+        [(k_hbm.at[last, :], ks), (v_hbm.at[last, :], vs), (q_hbm.at[last, :], qs)], sems
+    ):
+        copy.wait()
+    parts = []
+    for src in (ks, vs, qs):
+        parts.append(src[...].astype(f32)[8:16, :])
+    parts.append(parts[0])
+    out_ref[...] = jnp.concatenate(parts, axis=0).astype(bf16)
 
 
 def rotate_kernel(q_hbm, k_hbm, cos_ref, sin_ref, qo_ref, ko_ref, q_ref, k_ref, sems):
@@ -384,7 +397,14 @@
     idx = jnp.stack([me // (NZ * NQ), (me // NQ) % NZ, me % NQ]).astype(jnp.int32)
     dma = pltpu.SemaphoreType.DMA
     hyena = jnp.concatenate([hyena_k, hyena_v, hyena_q], axis=0)
-    rim = jnp.concatenate([hyena[(i + 1) * TOK - 8 : (i + 1) * TOK] for i in range(3)], axis=0)
+    rim = call(
+        rim_kernel,
+        sds((32, WIDTH), bf16),
+        (hyena_k, hyena_v, hyena_q),
+        scratch=[pltpu.VMEM((16, WIDTH), bf16)] * 3 + [dma((3,))],
+        hbm=(0, 1, 2),
+        vmem=60,
+    )
     halo = lax.ppermute(rim, "ctx", [(i, i + 1) for i in range(N_CTX - 1)])
 
     angles = (offsets[me] + jnp.arange(TOK, dtype=jnp.int32)).astype(f32)[:, None] * head_freqs(HEAD_DIM)[None, :]

time: 114 us -> 112 us (0.982)
  local copies, waits for them, and re-layouts: 2.86 us -> 0.66 us
  Pallas kernels: 12.6 us -> 14 us
  blocking collectives: 11.5 us -> 10.2 us
    slice x3 -> x0, local copies, waits for them, and re-layouts: 2.21 us -> none  [local(): hyena[(i + 1) * TOK - 8:(i + 1) * TOK]]
    pallas_call x13 -> x14, Pallas kernels: 12.6 us -> 14 us  [call(): pl.pallas_call(kernel, out_shape=out_shape, in_specs=specs, out_specs=out...]
    ppermute x2, waiting for transfers between devices: 10.6 us -> 9.25 us  [ahead_extra(): lax.ppermute(value, 'ctx', [(i, (i + (5 if i % 2 else 1)) % N_CTX) for i...]
    psum x1, blocking collectives: 11.5 us -> 10.2 us  [local(): total = lax.psum(squares, 'ch')]
where the time goes in v3:
time: 112 us; the launch traced here: 110 us
  starting transfers between devices  43.8 us (39%)
  waiting for transfers between devices  38.4 us (34%)
  Pallas kernels  14 us (12%)
  blocking collectives  10.2 us (9%)
  other arithmetic  2.33 us (2%)
    pallas_call x14, Pallas kernels, call(): pl.pallas_call(kernel, out_shape=out_shape, in_specs=specs, out_specs=out...  14 us
    ppermute x4, starting transfers between devices, ahead(): lax.ppermute(value, 'ctx', [(i, (i + steps) % N_CTX) for i in range(N_CTX)])  13.5 us
    ppermute x1, waiting for transfers between devices, local(): halo = lax.ppermute(rim, 'ctx', [(i, i + 1) for i in range(N_CTX - 1)])  11.7 us
    ppermute x2, starting transfers between devices, core_swap(): return lax.ppermute(value, 'ctx', [(i, i ^ 1) for i in range(N_CTX)])  11.2 us
    psum x1, blocking collectives, local(): total = lax.psum(squares, 'ch')  10.2 us
    ppermute x2, waiting for transfers between devices, ahead_extra(): lax.ppermute(value, 'ctx', [(i, (i + (5 if i % 2 else 1)) % N_CTX) for i...  9.25 us
    ppermute x4, waiting for transfers between devices, ahead(): lax.ppermute(value, 'ctx', [(i, (i + steps) % N_CTX) for i in range(N_CTX)])  8.95 us
    all_to_all x1, waiting for transfers between devices, local(): lax.all_to_all(state, 'ctx', 0, 0, tiled=True, axis_index_groups=z_groups())  6.45 us
  transfers between devices with their start and end apart: 12, of which 7 were waited for; matrix products, arithmetic and copies ran while one was open for 3% of the time, Pallas kernels for 9%

profile of v3, /device:TPU:6, one launch (start us, length us, event | category | flops | bytes accessed | tf_op | source)
XLA Modules:
  0.0 110.4 jit_solution(15912406558933402806)
XLA Ops:
  0.7 1.5 %shard_map.122 = bf16[32,1024]{1,0:T(8,128)(2,1)} custom-call(bf16[128,1024]{1,0:T(8,128)(2,1)} %k_hbm.2, bf16[128,1024]{1,0:T(8,128)(2,1)} %v_hbm.1, bf16[128,1024]{1,0:T(8,128)(2,1)} %q_hbm.2), custom_call_target="tpu_custom_call" | custom-call | flops 1000000 | bytes 1000000 | tf_op jit(solution)/shard_map/pallas_call | solution.py:39
  2.2 0.0 copy-start.8
  2.2 1.9 %collective-permute-start = (bf16[32,1024]{1,0:T(8,128)(2,1)}, bf16[32,1024]{1,0:T(8,128)(2,1)S(1)}, u32[]{:S(2)}, u32[]{:S(2)}) collective-permute-start(bf16[32,1024]{1,0:T(8,128)(2,1)} %shard_map.122), channel_id=1, source_target_pairs={{0,4},{4,8},{8,12},{12,16},{16,20},{20,24},{24,28},{28,32},{32,36}... | collective-permute-start | bytes 196616 | tf_op jit(solution)/shard_map/ppermute | solution.py:408
  4.1 1.2 %pad_maximum_fusion.h_ref = bf16[384,1024]{1,0:T(8,128)(2,1)S(1)} fusion(bf16[128,1024]{1,0:T(8,128)(2,1)} %q_hbm.2, bf16[128,1024]{1,0:T(8,128)(2,1)} %v_hbm.1, bf16[128,1024]{1,0:T(8,128)(2,1)} %k_hbm.2), kind=kLoop, calls=%fused_computation | loop fusion | flops 2359296 | bytes 1572864 | tf_op jit(solution)/shard_map/concatenate | solution.py:399
  5.3 0.0 copy-start.1
  5.3 0.0 copy-start.2
  5.4 1.9 %shard_map.123 = (f32[1024,128]{1,0:T(8,128)S(1)}, f32[1024,128]{1,0:T(8,128)S(1)}, f32[504,128]{1,0:T(8,128)S(1)}) custom-call(bf16[384,1024]{1,0:T(8,128)(2,1)S(1)} %pad_maximum_fusion.h_ref, f32[41,1024]{1,0:T(8,128)S(1)} %pad_maximum_fusion.1.p_ref), custom_call_target="tpu_custom_call" | custom-call | flops 1000000 | bytes 1000000 | tf_op jit(solution)/shard_map/pallas_call | solution.py:39
  7.3 0.0 copy-done.8
  7.3 0.6 dynamic_slice.3
  7.9 0.6 add_convert_fusion
  8.5 11.7 %collective-permute-done.halo_ref = bf16[32,1024]{1,0:T(8,128)(2,1)S(1)} collective-permute-done((bf16[32,1024]{1,0:T(8,128)(2,1)}, bf16[32,1024]{1,0:T(8,128)(2,1)S(1)}, u32[]{:S(2)}, u32[]{:S(2)}) %collective-permute-start) | collective-permute-done | bytes 65568 | tf_op jit(solution)/shard_map/ppermute | solution.py:408
  20.2 0.8 shard_map.124
  21.0 4.1 %all-to-all-start = ((bf16[8,128,128]{2,1,0:T(8,128)(2,1)}), bf16[8,128,128]{2,1,0:T(8,128)(2,1)S(1)}, u32[]{:S(2)}, u32[]{:S(2)}) async-start(bf16[8,128,128]{2,1,0:T(8,128)(2,1)} %get-tuple-element.26.f_ref), calls=%async_computation | async-start | bytes 524288 | tf_op jit(solution)/shard_map/all_to_all | solution.py:439
  25.1 0.3 fusion
  25.4 0.1 pad_maximum_fusion.2
  25.5 0.3 shard_map.126
  25.9 5.6 %collective-permute-start.2 = (bf16[128,1024]{1,0:T(8,128)(2,1)S(1)}, bf16[128,1024]{1,0:T(8,128)(2,1)S(1)}, u32[]{:S(2)}, u32[]{:S(2)}) collective-permute-start(bf16[128,1024]{1,0:T(8,128)(2,1)S(1)} %get-tuple-element.40.src_ref.k0_ref), channel_id=1, source_target_pairs={{0,8},{4,12},{8,16},{12,20},{16,24},{20,28},{24,32},{28,36},{32,40... | collective-permute-start | bytes 786440 | tf_op jit(solution)/shard_map/ppermute | solution.py:372
  31.5 0.1 pad_add_fusion.idx_ref
  31.6 6.4 %all-to-all-done.fz_ref = bf16[8,128,128]{2,1,0:T(8,128)(2,1)S(1)} async-done(((bf16[8,128,128]{2,1,0:T(8,128)(2,1)}), bf16[8,128,128]{2,1,0:T(8,128)(2,1)S(1)}, u32[]{:S(2)}, u32[]{:S(2)}) %all-to-all-start) | async-done | bytes 262176 | tf_op jit(solution)/shard_map/all_to_all | solution.py:439
  38.0 1.3 %shard_map.125 = (bf16[4,128,128]{2,1,0:T(8,128)(2,1)}, f32[128,128]{1,0:T(8,128)S(1)}) custom-call(s32[3]{0:T(128)S(1)} %pad_add_fusion.idx_ref, bf16[8,128,128]{2,1,0:T(8,128)(2,1)S(1)} %all-to-all-done.fz_ref, f32[504,128]{1,0:T(8,128)S(1)} %get-tuple-element.25.table_ref), custom_call_target="tpu_custom_call" | custom-call | flops 1000000 | bytes 1000000 | tf_op jit(solution)/shard_map/pallas_call | solution.py:39
  39.3 4.6 %all-to-all-start.1 = ((bf16[4,128,128]{2,1,0:T(8,128)(2,1)}), bf16[4,128,128]{2,1,0:T(8,128)(2,1)S(1)}, u32[]{:S(2)}, u32[]{:S(2)}) async-start(bf16[4,128,128]{2,1,0:T(8,128)(2,1)} %get-tuple-element.29), calls=%async_computation.1 | async-start | bytes 262144 | tf_op jit(solution)/shard_map/all_to_all | solution.py:446
  43.9 0.7 shard_map.128
  44.6 1.9 %collective-permute-start.1 = (bf16[128,1024]{1,0:T(8,128)(2,1)}, bf16[128,1024]{1,0:T(8,128)(2,1)S(1)}, u32[]{:S(2)}, u32[]{:S(2)}) collective-permute-start(bf16[128,1024]{1,0:T(8,128)(2,1)} %shard_map.128), channel_id=1, source_target_pairs={{0,4},{4,24},{8,12},{12,32},{16,20},{20,40},{24,28},{28,48},{32,36... | collective-permute-start | bytes 786440 | tf_op jit(solution)/shard_map/ppermute | solution.py:380
  46.5 1.3 %all-to-all-done.1.ux_ref = bf16[4,128,128]{2,1,0:T(8,128)(2,1)S(1)} async-done(((bf16[4,128,128]{2,1,0:T(8,128)(2,1)}), bf16[4,128,128]{2,1,0:T(8,128)(2,1)S(1)}, u32[]{:S(2)}, u32[]{:S(2)}) %all-to-all-start.1) | async-done | bytes 131104 | tf_op jit(solution)/shard_map/all_to_all | solution.py:446
  47.8 1.7 %shard_map.127 = bf16[4,128,128]{2,1,0:T(8,128)(2,1)} custom-call(s32[3]{0:T(128)S(1)} %pad_add_fusion.idx_ref, bf16[4,128,128]{2,1,0:T(8,128)(2,1)S(1)} %all-to-all-done.1.ux_ref, f32[128,128]{1,0:T(8,128)S(1)} %get-tuple-element.30.before_ref, bf16[8,128,128]{2,1,0:T(8,128)(2,1)} %get-tuple-element.26.f_ref, f32[504,128]{1,0:T(8,128)S(1)} %get-tuple-element.25.table_ref), custom_call_target="tpu_custom_call" | custom-call | flops 1000000 | bytes 1000000 | tf_op jit(solution)/shard_map/pallas_call | solution.py:39
  49.5 4.7 %all-to-all-start.2 = ((bf16[4,128,128]{2,1,0:T(8,128)(2,1)}), bf16[4,128,128]{2,1,0:T(8,128)(2,1)S(1)}, u32[]{:S(2)}, u32[]{:S(2)}) async-start(bf16[4,128,128]{2,1,0:T(8,128)(2,1)} %shard_map.127), calls=%async_computation.2 | async-start | bytes 262144 | tf_op jit(solution)/shard_map/all_to_all | solution.py:452
  54.2 2.8 %collective-permute-start.3 = (bf16[128,1024]{1,0:T(8,128)(2,1)S(1)}, bf16[128,1024]{1,0:T(8,128)(2,1)S(1)}, u32[]{:S(2)}, u32[]{:S(2)}) collective-permute-start(bf16[128,1024]{1,0:T(8,128)(2,1)S(1)} %shard_map.130), channel_id=1, source_target_pairs={{0,16},{4,20},{8,24},{12,28},{16,32},{20,36},{24,40},{28,44},{32,4... | collective-permute-start | bytes 786440 | tf_op jit(solution)/shard_map/ppermute | solution.py:372
  57.0 0.0 collective-permute-done.2.a_ref.k1_ref
  57.0 5.5 %collective-permute-done.1.k5_ref = bf16[128,1024]{1,0:T(8,128)(2,1)S(1)} collective-permute-done((bf16[128,1024]{1,0:T(8,128)(2,1)}, bf16[128,1024]{1,0:T(8,128)(2,1)S(1)}, u32[]{:S(2)}, u32[]{:S(2)}) %collective-permute-start.1) | collective-permute-done | bytes 262176 | tf_op jit(solution)/shard_map/ppermute | solution.py:380
  62.6 0.7 all-to-all-done.2.yq_ref
  63.3 2.1 %shard_map.129.v0_ref = bf16[128,1024]{1,0:T(8,128)(2,1)} custom-call(s32[3]{0:T(128)S(1)} %pad_add_fusion.idx_ref, bf16[4,128,128]{2,1,0:T(8,128)(2,1)S(1)} %all-to-all-done.2.yq_ref, f32[504,128]{1,0:T(8,128)S(1)} %get-tuple-element.25.table_ref, f32[32,128]{1,0:T(8,128)S(1)} %get-tuple-element.34.em_ref, f32[1024,128]{1,0:T(8,128)S(1)} %get-tuple-element.35.l_ref, ...), custom_call_target="tpu_custom_call" | custom-call | flops 1000000 | bytes 1000000 | tf_op jit(solution)/shard_map/pallas_call | solution.py:39
  65.4 3.1 %collective-permute-start.5 = (bf16[128,1024]{1,0:T(8,128)(2,1)}, bf16[128,1024]{1,0:T(8,128)(2,1)S(1)}, u32[]{:S(2)}, u32[]{:S(2)}) collective-permute-start(bf16[128,1024]{1,0:T(8,128)(2,1)} %shard_map.129.v0_ref), channel_id=1, source_target_pairs={{0,8},{4,12},{8,16},{12,20},{16,24},{20,28},{24,32},{28,36},{32,40... | collective-permute-start | bytes 786440 | tf_op jit(solution)/shard_map/ppermute | solution.py:372
  68.5 1.9 %collective-permute-start.6 = (bf16[128,1024]{1,0:T(8,128)(2,1)}, bf16[128,1024]{1,0:T(8,128)(2,1)S(1)}, u32[]{:S(2)}, u32[]{:S(2)}) collective-permute-start(bf16[128,1024]{1,0:T(8,128)(2,1)} %shard_map.129.v0_ref), channel_id=1, source_target_pairs={{0,4},{4,24},{8,12},{12,32},{16,20},{20,40},{24,28},{28,48},{32,36... | collective-permute-start | bytes 786440 | tf_op jit(solution)/shard_map/ppermute | solution.py:380
  70.4 2.0 %collective-permute-start.7 = (bf16[128,1024]{1,0:T(8,128)(2,1)}, bf16[128,1024]{1,0:T(8,128)(2,1)S(1)}, u32[]{:S(2)}, u32[]{:S(2)}) collective-permute-start(bf16[128,1024]{1,0:T(8,128)(2,1)} %shard_map.129.v0_ref), channel_id=1, source_target_pairs={{0,16},{4,20},{8,24},{12,28},{16,32},{20,36},{24,40},{28,44},{32,4... | collective-permute-start | bytes 786440 | tf_op jit(solution)/shard_map/ppermute | solution.py:372
  72.4 0.0 collective-permute-done.3.b_ref.k2_ref
  72.4 0.0 copy-start
  72.5 8.1 %collective-permute-start.4 = (bf16[2,128,1024]{2,1,0:T(8,128)(2,1)S(1)}, bf16[2,128,1024]{2,1,0:T(8,128)(2,1)S(1)}, u32[]{:S(2)}, u32[]{:S(2)}) collective-permute-start(bf16[2,128,1024]{2,1,0:T(8,128)(2,1)S(1)} %shard_map.131), channel_id=1, source_target_pairs={{0,4},{4,0},{8,12},{12,8},{16,20},{20,16},{24,28},{28,24},{32,36},... | collective-permute-start | bytes 1572872 | tf_op jit(solution)/shard_map/ppermute | solution.py:376
  80.6 8.9 %collective-permute-done.5.a_ref.v1_ref = bf16[128,1024]{1,0:T(8,128)(2,1)S(1)} collective-permute-done((bf16[128,1024]{1,0:T(8,128)(2,1)}, bf16[128,1024]{1,0:T(8,128)(2,1)S(1)}, u32[]{:S(2)}, u32[]{:S(2)}) %collective-permute-start.5) | collective-permute-done | bytes 262176 | tf_op jit(solution)/shard_map/ppermute | solution.py:372
  89.5 3.7 %collective-permute-done.6.v5_ref = bf16[128,1024]{1,0:T(8,128)(2,1)S(1)} collective-permute-done((bf16[128,1024]{1,0:T(8,128)(2,1)}, bf16[128,1024]{1,0:T(8,128)(2,1)S(1)}, u32[]{:S(2)}, u32[]{:S(2)}) %collective-permute-start.6) | collective-permute-done | bytes 262176 | tf_op jit(solution)/shard_map/ppermute | solution.py:380
  93.3 0.0 collective-permute-done.7.b_ref.v2_ref
  93.3 3.1 %collective-permute-start.8 = (bf16[2,128,1024]{2,1,0:T(8,128)(2,1)S(1)}, bf16[2,128,1024]{2,1,0:T(8,128)(2,1)S(1)}, u32[]{:S(2)}, u32[]{:S(2)}) collective-permute-start(bf16[2,128,1024]{2,1,0:T(8,128)(2,1)S(1)} %shard_map.133), channel_id=1, source_target_pairs={{0,4},{4,0},{8,12},{12,8},{16,20},{20,16},{24,28},{28,24},{32,36},... | collective-permute-start | bytes 1572872 | tf_op jit(solution)/shard_map/ppermute | solution.py:376
  96.4 0.0 collective-permute-done.4.swap_ref
  96.5 2.2 %shard_map.132 = (bf16[8,128,768]{2,1,0:T(8,128)(2,1)S(1)}, f32[128,128]{1,0:T(8,128)S(1)}) custom-call(s32[3]{0:T(128)S(1)} %pad_add_fusion.idx_ref, s32[1,6]{1,0:T(1,128)S(1)} %copy-done.4, bf16[128,1024]{1,0:T(8,128)(2,1)S(1)} %get-tuple-element.37.q_ref, bf16[128,1024]{1,0:T(8,128)(2,1)S(1)} %get-tuple-element.40.src_ref.k0_ref, ...), custom_call_target="tpu_custom_call" | custom-call | flops 1000000 | bytes 1000000 | tf_op jit(solution)/shard_map/pallas_call | solution.py:39
  98.7 0.0 collective-permute-done.8.swap_ref
  98.7 0.0 copy-start.3
  98.7 0.7 shard_map.134
  99.4 10.2 %psum.7.sq_ref = f32[1,128]{1,0:T(1,128)S(1)} all-reduce(f32[1,128]{1,0:T(1,128)S(1)} %get-tuple-element.47), channel_id=1, replica_groups=mesh['ctx'=128,'ch'=4] {'ch'}, use_global_device_ids=true, to_apply=%region_0.1 | all-reduce | flops 128 | bytes 1024 | tf_op jit(solution)/shard_map/psum | solution.py:477
  109.6 0.8 shard_map.135
  (18 shorter events, 0.2 us)
Async XLA Ops:
  0.6 4.7 %copy-start.7 = (f32[3,3,1024]{2,1,0:T(4,128)S(1)}, f32[3,3,1024]{2,1,0:T(4,128)}, u32[]{:S(2)}) copy-start(f32[3,3,1024]{2,1,0:T(4,128)} %param.14) | copy-start | bytes 110596
  0.6 4.7 %copy-start.5 = (f32[16,1024]{1,0:T(8,128)S(1)}, f32[16,1024]{1,0:T(8,128)}, u32[]{:S(2)}) copy-start(f32[16,1024]{1,0:T(8,128)} %param.15) | copy-start | bytes 196612
  0.7 4.7 %copy-start.6 = (f32[16,1024]{1,0:T(8,128)S(1)}, f32[16,1024]{1,0:T(8,128)}, u32[]{:S(2)}) copy-start(f32[16,1024]{1,0:T(8,128)} %param.16) | copy-start | bytes 196612
  2.2 5.1 %copy-start.8 = (s32[128]{0:T(128)S(1)}, s32[128]{0:T(128)}, u32[]{:S(2)}) copy-start(s32[128]{0:T(128)} %param.19) | copy-start | bytes 1540
  2.2 18.1 %collective-permute-start = (bf16[32,1024]{1,0:T(8,128)(2,1)}, bf16[32,1024]{1,0:T(8,128)(2,1)S(1)}, u32[]{:S(2)}, u32[]{:S(2)}) collective-permute-start(bf16[32,1024]{1,0:T(8,128)(2,1)} %shard_map.122), channel_id=1, source_target_pairs={{0,4},{4,8},{8,12},{12,16},{16,20},{20,24},{24,28},{28,32},{32,36}... | collective-permute-start | bytes 196616 | tf_op jit(solution)/shard_map/ppermute | solution.py:408
  5.3 20.2 %copy-start.1 = (bf16[128,1024]{1,0:T(8,128)(2,1)S(1)}, bf16[128,1024]{1,0:T(8,128)(2,1)}, u32[]{:S(2)}) copy-start(bf16[128,1024]{1,0:T(8,128)(2,1)} %q_hbm.3) | copy-start | bytes 786436
  5.3 20.2 %copy-start.2 = (bf16[128,1024]{1,0:T(8,128)(2,1)S(1)}, bf16[128,1024]{1,0:T(8,128)(2,1)}, u32[]{:S(2)}) copy-start(bf16[128,1024]{1,0:T(8,128)(2,1)} %k_hbm.3) | copy-start | bytes 786436
  21.0 17.0 %all-to-all-start = ((bf16[8,128,128]{2,1,0:T(8,128)(2,1)}), bf16[8,128,128]{2,1,0:T(8,128)(2,1)S(1)}, u32[]{:S(2)}, u32[]{:S(2)}) async-start(bf16[8,128,128]{2,1,0:T(8,128)(2,1)} %get-tuple-element.26.f_ref), calls=%async_computation | async-start | bytes 524288 | tf_op jit(solution)/shard_map/all_to_all | solution.py:439
  25.9 31.2 %collective-permute-start.2 = (bf16[128,1024]{1,0:T(8,128)(2,1)S(1)}, bf16[128,1024]{1,0:T(8,128)(2,1)S(1)}, u32[]{:S(2)}, u32[]{:S(2)}) collective-permute-start(bf16[128,1024]{1,0:T(8,128)(2,1)S(1)} %get-tuple-element.40.src_ref.k0_ref), channel_id=1, source_target_pairs={{0,8},{4,12},{8,16},{12,20},{16,24},{20,28},{24,32},{28,36},{32,40... | collective-permute-start | bytes 786440 | tf_op jit(solution)/shard_map/ppermute | solution.py:372
  39.3 8.5 %all-to-all-start.1 = ((bf16[4,128,128]{2,1,0:T(8,128)(2,1)}), bf16[4,128,128]{2,1,0:T(8,128)(2,1)S(1)}, u32[]{:S(2)}, u32[]{:S(2)}) async-start(bf16[4,128,128]{2,1,0:T(8,128)(2,1)} %get-tuple-element.29), calls=%async_computation.1 | async-start | bytes 262144 | tf_op jit(solution)/shard_map/all_to_all | solution.py:446
  44.6 17.9 %collective-permute-start.1 = (bf16[128,1024]{1,0:T(8,128)(2,1)}, bf16[128,1024]{1,0:T(8,128)(2,1)S(1)}, u32[]{:S(2)}, u32[]{:S(2)}) collective-permute-start(bf16[128,1024]{1,0:T(8,128)(2,1)} %shard_map.128), channel_id=1, source_target_pairs={{0,4},{4,24},{8,12},{12,32},{16,20},{20,40},{24,28},{28,48},{32,36... | collective-permute-start | bytes 786440 | tf_op jit(solution)/shard_map/ppermute | solution.py:380
  49.5 13.8 %all-to-all-start.2 = ((bf16[4,128,128]{2,1,0:T(8,128)(2,1)}), bf16[4,128,128]{2,1,0:T(8,128)(2,1)S(1)}, u32[]{:S(2)}, u32[]{:S(2)}) async-start(bf16[4,128,128]{2,1,0:T(8,128)(2,1)} %shard_map.127), calls=%async_computation.2 | async-start | bytes 262144 | tf_op jit(solution)/shard_map/all_to_all | solution.py:452
  54.2 18.2 %collective-permute-start.3 = (bf16[128,1024]{1,0:T(8,128)(2,1)S(1)}, bf16[128,1024]{1,0:T(8,128)(2,1)S(1)}, u32[]{:S(2)}, u32[]{:S(2)}) collective-permute-start(bf16[128,1024]{1,0:T(8,128)(2,1)S(1)} %shard_map.130), channel_id=1, source_target_pairs={{0,16},{4,20},{8,24},{12,28},{16,32},{20,36},{24,40},{28,44},{32,4... | collective-permute-start | bytes 786440 | tf_op jit(solution)/shard_map/ppermute | solution.py:372
  63.3 33.2 %copy-start.4 = (s32[1,6]{1,0:T(1,128)S(1)}, s32[1,6]{1,0:T(1,128)}, u32[]{:S(2)}) copy-start(s32[1,6]{1,0:T(1,128)} %mask_ref.1) | copy-start | bytes 76
  65.4 24.2 %collective-permute-start.5 = (bf16[128,1024]{1,0:T(8,128)(2,1)}, bf16[128,1024]{1,0:T(8,128)(2,1)S(1)}, u32[]{:S(2)}, u32[]{:S(2)}) collective-permute-start(bf16[128,1024]{1,0:T(8,128)(2,1)} %shard_map.129.v0_ref), channel_id=1, source_target_pairs={{0,8},{4,12},{8,16},{12,20},{16,24},{20,28},{24,32},{28,36},{32,40... | collective-permute-start | bytes 786440 | tf_op jit(solution)/shard_map/ppermute | solution.py:372
  68.5 24.8 %collective-permute-start.6 = (bf16[128,1024]{1,0:T(8,128)(2,1)}, bf16[128,1024]{1,0:T(8,128)(2,1)S(1)}, u32[]{:S(2)}, u32[]{:S(2)}) collective-permute-start(bf16[128,1024]{1,0:T(8,128)(2,1)} %shard_map.129.v0_ref), channel_id=1, source_target_pairs={{0,4},{4,24},{8,12},{12,32},{16,20},{20,40},{24,28},{28,48},{32,36... | collective-permute-start | bytes 786440 | tf_op jit(solution)/shard_map/ppermute | solution.py:380
  70.4 22.9 %collective-permute-start.7 = (bf16[128,1024]{1,0:T(8,128)(2,1)}, bf16[128,1024]{1,0:T(8,128)(2,1)S(1)}, u32[]{:S(2)}, u32[]{:S(2)}) collective-permute-start(bf16[128,1024]{1,0:T(8,128)(2,1)} %shard_map.129.v0_ref), channel_id=1, source_target_pairs={{0,16},{4,20},{8,24},{12,28},{16,32},{20,36},{24,40},{28,44},{32,4... | collective-permute-start | bytes 786440 | tf_op jit(solution)/shard_map/ppermute | solution.py:372
  72.4 26.2 %copy-start = (bf16[128,1024]{1,0:T(8,128)(2,1)S(1)}, bf16[128,1024]{1,0:T(8,128)(2,1)}, u32[]{:S(2)}) copy-start(bf16[128,1024]{1,0:T(8,128)(2,1)} %shard_map.129.v0_ref) | copy-start | bytes 786436
  72.5 24.0 %collective-permute-start.4 = (bf16[2,128,1024]{2,1,0:T(8,128)(2,1)S(1)}, bf16[2,128,1024]{2,1,0:T(8,128)(2,1)S(1)}, u32[]{:S(2)}, u32[]{:S(2)}) collective-permute-start(bf16[2,128,1024]{2,1,0:T(8,128)(2,1)S(1)} %shard_map.131), channel_id=1, source_target_pairs={{0,4},{4,0},{8,12},{12,8},{16,20},{20,16},{24,28},{28,24},{32,36},... | collective-permute-start | bytes 1572872 | tf_op jit(solution)/shard_map/ppermute | solution.py:376
  93.3 5.4 %collective-permute-start.8 = (bf16[2,128,1024]{2,1,0:T(8,128)(2,1)S(1)}, bf16[2,128,1024]{2,1,0:T(8,128)(2,1)S(1)}, u32[]{:S(2)}, u32[]{:S(2)}) collective-permute-start(bf16[2,128,1024]{2,1,0:T(8,128)(2,1)S(1)} %shard_map.133), channel_id=1, source_target_pairs={{0,4},{4,0},{8,12},{12,8},{16,20},{20,16},{24,28},{28,24},{32,36},... | collective-permute-start | bytes 1572872 | tf_op jit(solution)/shard_map/ppermute | solution.py:376
  98.7 10.9 %copy-start.3 = (f32[1024]{0:T(1024)S(1)}, f32[1024]{0:T(1024)}, u32[]{:S(2)}) copy-start(f32[1024]{0:T(1024)} %param.21) | copy-start | bytes 12292

commit v4 on v3

--- a/solution.py
+++ b/solution.py
@@ -180,7 +180,7 @@
         f0_ref[m * ROWS : (m + 1) * ROWS, :] = state[m]
 
 
-def edge_kernel(halo_ref, table_ref, f_ref, em_ref, hs):
+def edge_kernel(halo_ref, table_ref, f_ref, em_ref, own_ref, hs):
     f0_ref = table_ref.at[T_STATE:T_RATE]
     rr_ref = table_ref.at[T_RATE:T_GAIN]
     gg_ref = table_ref.at[T_GAIN:T_TAP]
@@ -220,6 +220,7 @@
                 + gain * (jnp.exp(rate * -127.0) * m0 + jnp.exp(rate * -126.0) * m1)
             )
         both = jnp.concatenate(both, axis=0).astype(bf16)
+        own_ref[i * 2 * ROWS : (i + 1) * 2 * ROWS, :] = both
         for copy in range(NZ):
             f_ref[copy, i * 2 * ROWS : (i + 1) * 2 * ROWS, :] = both
 
@@ -249,13 +250,13 @@
         if i < NX - 1:
             running = d * running + ux_ref[i].astype(f32)
     before = before_ref[...] + jnp.exp(rate * (z * -(TOK * NQ)).astype(f32)) * carry
-    after = jnp.exp(rate * -float(TOK * NQ)) * before + f_ref[0].astype(f32)
+    after = jnp.exp(rate * -float(TOK * NQ)) * before + f_ref[...].astype(f32)
     before, after = before.astype(bf16), after.astype(bf16)
     for i in range(NQ):
         y_ref[i] = jnp.where(q < i, after, before)
 
 
-def out_kernel(idx_ref, yq_ref, table_ref, em_ref, l_ref, fq_ref, out_ref, cs, ys):
+def out_kernel(idx_ref, yq_ref, table_ref, em_ref, l_ref, fq_ref, out_ref, ys):
     q = idx_ref[2]
     rate = table_ref[T_RATE:T_GAIN, :]
     own = tree_sum(
@@ -276,15 +277,13 @@
     ys[0:ROWS, :] = q0 * tree_sum(state)
     state = [decay[m] * state[m] + tile(gain_all, m) * m1 for m in range(MODES)]
     ys[ROWS : 2 * ROWS, :] = q1 * tree_sum(state)
-    for m in range(MODES):
-        cs[m * ROWS : (m + 1) * ROWS, :] = tile(decay_all, m)
-    unroll = 6
+    unroll = 18
 
     def step(it, carry_now):
         state = list(carry_now)
         for o in range(unroll):
             now = tok_rows(it * unroll + 2 + o)
-            state = [cs[m * ROWS : (m + 1) * ROWS, :] * state[m] for m in range(MODES)]
+            state = [decay[m] * state[m] for m in range(MODES)]
             ys[now, :] = fq_ref[now, :] * (l_ref[now, :] + tree_sum(state))
         return tuple(state)
 
@@ -430,9 +429,13 @@
         (hyena, params),
         scratch=[pltpu.VMEM((TOK * ROWS, LANES), f32)] * 3 + [pltpu.VMEM((MODES * ROWS, LANES), f32)],
     )
-    state, em = call(
+    state, em, own_state = call(
         edge_kernel,
-        [sds((NZ, MODES * ROWS, LANES), bf16), sds((4 * ROWS, LANES), f32)],
+        [
+            sds((NZ, MODES * ROWS, LANES), bf16),
+            sds((4 * ROWS, LANES), f32),
+            sds((MODES * ROWS, LANES), bf16),
+        ],
         (halo, table),
         scratch=[pltpu.VMEM((24 * ROWS, LANES), f32)],
     )
@@ -445,7 +448,7 @@
     k_extra = ahead_extra(call(copy_kernel, sds((TOK, WIDTH), bf16), (k_late,), flops=5_000_000_000))
     along_x = lax.all_to_all(column, "ctx", 0, 0, tiled=True, axis_index_groups=x_groups())
     classes = call(
-        x_kernel, sds((NQ, MODES * ROWS, LANES), bf16), (idx, along_x, before, state, table), smem=(0,)
+        x_kernel, sds((NQ, MODES * ROWS, LANES), bf16), (idx, along_x, before, own_state, table), smem=(0,)
     )
     classes, k_late = lax.optimization_barrier((classes, k_late))
     k_four = ahead(call(copy_kernel, sds((TOK, WIDTH), bf16), (k_late,), flops=5_000_000_000), 4)
@@ -455,7 +458,7 @@
         out_kernel,
         sds((TOK, WIDTH), bf16),
         (idx, quad, table, em, l_rest, feat_q),
-        scratch=[pltpu.VMEM((MODES * ROWS, LANES), f32), pltpu.VMEM((TOK * ROWS, LANES), f32)],
+        scratch=[pltpu.VMEM((TOK * ROWS, LANES), f32)],
         smem=(0,),
     )
     v_two, v_four, v_extra = window_far(hyena_out)

time: 112 us -> 111 us (level)
  no operation moved by 1% of the time
where the time goes in v4:
time: 111 us; the launch traced here: 110 us
  starting transfers between devices  43.9 us (40%)
  waiting for transfers between devices  38.4 us (35%)
  Pallas kernels  13.5 us (12%)
  blocking collectives  9.79 us (9%)
  other arithmetic  2.33 us (2%)
    ppermute x4, starting transfers between devices, ahead(): lax.ppermute(value, 'ctx', [(i, (i + steps) % N_CTX) for i in range(N_CTX)])  13.6 us
    pallas_call x14, Pallas kernels, call(): pl.pallas_call(kernel, out_shape=out_shape, in_specs=specs, out_specs=out...  13.5 us
    ppermute x1, waiting for transfers between devices, local(): halo = lax.ppermute(rim, 'ctx', [(i, i + 1) for i in range(N_CTX - 1)])  11.7 us
    ppermute x2, starting transfers between devices, core_swap(): return lax.ppermute(value, 'ctx', [(i, i ^ 1) for i in range(N_CTX)])  11.3 us
    ppermute x2, waiting for transfers between devices, ahead_extra(): lax.ppermute(value, 'ctx', [(i, (i + (5 if i % 2 else 1)) % N_CTX) for i...  10.3 us
    psum x1, blocking collectives, local(): total = lax.psum(squares, 'ch')  9.79 us
    ppermute x4, waiting for transfers between devices, ahead(): lax.ppermute(value, 'ctx', [(i, (i + steps) % N_CTX) for i in range(N_CTX)])  8.32 us
    all_to_all x1, waiting for transfers between devices, local(): lax.all_to_all(state, 'ctx', 0, 0, tiled=True, axis_index_groups=z_groups())  6.45 us
  transfers between devices with their start and end apart: 12, of which 7 were waited for; matrix products, arithmetic and copies ran while one was open for 3% of the time, Pallas kernels for 9%

profile of v4, /device:TPU:6, one launch (start us, length us, event | category | flops | bytes accessed | tf_op | source)
XLA Modules:
  0.0 109.7 jit_solution(18039847197240326186)
XLA Ops:
  0.7 1.5 %shard_map.122 = bf16[32,1024]{1,0:T(8,128)(2,1)} custom-call(bf16[128,1024]{1,0:T(8,128)(2,1)} %k_hbm.2, bf16[128,1024]{1,0:T(8,128)(2,1)} %v_hbm.1, bf16[128,1024]{1,0:T(8,128)(2,1)} %q_hbm.2), custom_call_target="tpu_custom_call" | custom-call | flops 1000000 | bytes 1000000 | tf_op jit(solution)/shard_map/pallas_call | solution.py:39
  2.2 0.0 copy-start.8
  2.2 1.9 %collective-permute-start = (bf16[32,1024]{1,0:T(8,128)(2,1)}, bf16[32,1024]{1,0:T(8,128)(2,1)S(1)}, u32[]{:S(2)}, u32[]{:S(2)}) collective-permute-start(bf16[32,1024]{1,0:T(8,128)(2,1)} %shard_map.122), channel_id=1, source_target_pairs={{0,4},{4,8},{8,12},{12,16},{16,20},{20,24},{24,28},{28,32},{32,36}... | collective-permute-start | bytes 196616 | tf_op jit(solution)/shard_map/ppermute | solution.py:407
  4.1 1.2 %pad_maximum_fusion.h_ref = bf16[384,1024]{1,0:T(8,128)(2,1)S(1)} fusion(bf16[128,1024]{1,0:T(8,128)(2,1)} %q_hbm.2, bf16[128,1024]{1,0:T(8,128)(2,1)} %v_hbm.1, bf16[128,1024]{1,0:T(8,128)(2,1)} %k_hbm.2), kind=kLoop, calls=%fused_computation | loop fusion | flops 2359296 | bytes 1572864 | tf_op jit(solution)/shard_map/concatenate | solution.py:398
  5.3 0.0 copy-start.1
  5.3 0.0 copy-start.2
  5.4 1.9 %shard_map.123 = (f32[1024,128]{1,0:T(8,128)S(1)}, f32[1024,128]{1,0:T(8,128)S(1)}, f32[504,128]{1,0:T(8,128)S(1)}) custom-call(bf16[384,1024]{1,0:T(8,128)(2,1)S(1)} %pad_maximum_fusion.h_ref, f32[41,1024]{1,0:T(8,128)S(1)} %pad_maximum_fusion.1.p_ref), custom_call_target="tpu_custom_call" | custom-call | flops 1000000 | bytes 1000000 | tf_op jit(solution)/shard_map/pallas_call | solution.py:39
  7.3 0.6 dynamic_slice.3
  7.9 0.6 add_convert_fusion
  8.5 11.7 %collective-permute-done.halo_ref = bf16[32,1024]{1,0:T(8,128)(2,1)S(1)} collective-permute-done((bf16[32,1024]{1,0:T(8,128)(2,1)}, bf16[32,1024]{1,0:T(8,128)(2,1)S(1)}, u32[]{:S(2)}, u32[]{:S(2)}) %collective-permute-start) | collective-permute-done | bytes 65568 | tf_op jit(solution)/shard_map/ppermute | solution.py:407
  20.2 0.8 shard_map.124
  21.0 4.1 %all-to-all-start = ((bf16[8,128,128]{2,1,0:T(8,128)(2,1)}), bf16[8,128,128]{2,1,0:T(8,128)(2,1)S(1)}, u32[]{:S(2)}, u32[]{:S(2)}) async-start(bf16[8,128,128]{2,1,0:T(8,128)(2,1)} %get-tuple-element.27), calls=%async_computation | async-start | bytes 524288 | tf_op jit(solution)/shard_map/all_to_all | solution.py:442
  25.1 0.3 fusion
  25.4 0.1 pad_maximum_fusion.2
  25.5 0.0 copy-done.1
  25.5 0.3 shard_map.126
  25.9 5.6 %collective-permute-start.2 = (bf16[128,1024]{1,0:T(8,128)(2,1)S(1)}, bf16[128,1024]{1,0:T(8,128)(2,1)S(1)}, u32[]{:S(2)}, u32[]{:S(2)}) collective-permute-start(bf16[128,1024]{1,0:T(8,128)(2,1)S(1)} %get-tuple-element.42.src_ref.k0_ref), channel_id=1, source_target_pairs={{0,8},{4,12},{8,16},{12,20},{16,24},{20,28},{24,32},{28,36},{32,40... | collective-permute-start | bytes 786440 | tf_op jit(solution)/shard_map/ppermute | solution.py:371
  31.5 0.1 pad_add_fusion.idx_ref
  31.6 6.4 %all-to-all-done.fz_ref = bf16[8,128,128]{2,1,0:T(8,128)(2,1)S(1)} async-done(((bf16[8,128,128]{2,1,0:T(8,128)(2,1)}), bf16[8,128,128]{2,1,0:T(8,128)(2,1)S(1)}, u32[]{:S(2)}, u32[]{:S(2)}) %all-to-all-start) | async-done | bytes 262176 | tf_op jit(solution)/shard_map/all_to_all | solution.py:442
  38.0 1.3 %shard_map.125 = (bf16[4,128,128]{2,1,0:T(8,128)(2,1)}, f32[128,128]{1,0:T(8,128)S(1)}) custom-call(s32[3]{0:T(128)S(1)} %pad_add_fusion.idx_ref, bf16[8,128,128]{2,1,0:T(8,128)(2,1)S(1)} %all-to-all-done.fz_ref, f32[504,128]{1,0:T(8,128)S(1)} %get-tuple-element.26.table_ref), custom_call_target="tpu_custom_call" | custom-call | flops 1000000 | bytes 1000000 | tf_op jit(solution)/shard_map/pallas_call | solution.py:39
  39.3 4.6 %all-to-all-start.1 = ((bf16[4,128,128]{2,1,0:T(8,128)(2,1)}), bf16[4,128,128]{2,1,0:T(8,128)(2,1)S(1)}, u32[]{:S(2)}, u32[]{:S(2)}) async-start(bf16[4,128,128]{2,1,0:T(8,128)(2,1)} %get-tuple-element.30), calls=%async_computation.1 | async-start | bytes 262144 | tf_op jit(solution)/shard_map/all_to_all | solution.py:449
  43.9 0.7 shard_map.128
  44.6 1.9 %collective-permute-start.1 = (bf16[128,1024]{1,0:T(8,128)(2,1)}, bf16[128,1024]{1,0:T(8,128)(2,1)S(1)}, u32[]{:S(2)}, u32[]{:S(2)}) collective-permute-start(bf16[128,1024]{1,0:T(8,128)(2,1)} %shard_map.128), channel_id=1, source_target_pairs={{0,4},{4,24},{8,12},{12,32},{16,20},{20,40},{24,28},{28,48},{32,36... | collective-permute-start | bytes 786440 | tf_op jit(solution)/shard_map/ppermute | solution.py:379
  46.6 1.3 %all-to-all-done.1.ux_ref = bf16[4,128,128]{2,1,0:T(8,128)(2,1)S(1)} async-done(((bf16[4,128,128]{2,1,0:T(8,128)(2,1)}), bf16[4,128,128]{2,1,0:T(8,128)(2,1)S(1)}, u32[]{:S(2)}, u32[]{:S(2)}) %all-to-all-start.1) | async-done | bytes 131104 | tf_op jit(solution)/shard_map/all_to_all | solution.py:449
  47.8 1.3 %shard_map.127 = bf16[4,128,128]{2,1,0:T(8,128)(2,1)} custom-call(s32[3]{0:T(128)S(1)} %pad_add_fusion.idx_ref, bf16[4,128,128]{2,1,0:T(8,128)(2,1)S(1)} %all-to-all-done.1.ux_ref, f32[128,128]{1,0:T(8,128)S(1)} %get-tuple-element.31.before_ref, bf16[128,128]{1,0:T(8,128)(2,1)S(1)} %get-tuple-element.32.f_ref, f32[504,128]{1,0:T(8,128)S(1)} %get-tuple-element.26.table_ref), custom_call_target="tpu_custom_call" | custom-call | flops 1000000 | bytes 1000000 | tf_op jit(solution)/shard_map/pallas_call | solution.py:39
  49.1 4.7 %all-to-all-start.2 = ((bf16[4,128,128]{2,1,0:T(8,128)(2,1)}), bf16[4,128,128]{2,1,0:T(8,128)(2,1)S(1)}, u32[]{:S(2)}, u32[]{:S(2)}) async-start(bf16[4,128,128]{2,1,0:T(8,128)(2,1)} %shard_map.127), calls=%async_computation.2 | async-start | bytes 262144 | tf_op jit(solution)/shard_map/all_to_all | solution.py:455
  53.8 2.8 %collective-permute-start.3 = (bf16[128,1024]{1,0:T(8,128)(2,1)S(1)}, bf16[128,1024]{1,0:T(8,128)(2,1)S(1)}, u32[]{:S(2)}, u32[]{:S(2)}) collective-permute-start(bf16[128,1024]{1,0:T(8,128)(2,1)S(1)} %shard_map.130), channel_id=1, source_target_pairs={{0,16},{4,20},{8,24},{12,28},{16,32},{20,36},{24,40},{28,44},{32,4... | collective-permute-start | bytes 786440 | tf_op jit(solution)/shard_map/ppermute | solution.py:371
  56.6 0.0 collective-permute-done.2.a_ref.k1_ref
  56.6 6.0 %collective-permute-done.1.k5_ref = bf16[128,1024]{1,0:T(8,128)(2,1)S(1)} collective-permute-done((bf16[128,1024]{1,0:T(8,128)(2,1)}, bf16[128,1024]{1,0:T(8,128)(2,1)S(1)}, u32[]{:S(2)}, u32[]{:S(2)}) %collective-permute-start.1) | collective-permute-done | bytes 262176 | tf_op jit(solution)/shard_map/ppermute | solution.py:379
  62.6 0.4 all-to-all-done.2.yq_ref
  63.0 2.0 %shard_map.129.v0_ref = bf16[128,1024]{1,0:T(8,128)(2,1)} custom-call(s32[3]{0:T(128)S(1)} %pad_add_fusion.idx_ref, bf16[4,128,128]{2,1,0:T(8,128)(2,1)S(1)} %all-to-all-done.2.yq_ref, f32[504,128]{1,0:T(8,128)S(1)} %get-tuple-element.26.table_ref, f32[32,128]{1,0:T(8,128)S(1)} %get-tuple-element.36.em_ref, f32[1024,128]{1,0:T(8,128)S(1)} %get-tuple-element.37.l_ref, ...), custom_call_target="tpu_custom_call" | custom-call | flops 1000000 | bytes 1000000 | tf_op jit(solution)/shard_map/pallas_call | solution.py:39
  65.0 3.2 %collective-permute-start.5 = (bf16[128,1024]{1,0:T(8,128)(2,1)}, bf16[128,1024]{1,0:T(8,128)(2,1)S(1)}, u32[]{:S(2)}, u32[]{:S(2)}) collective-permute-start(bf16[128,1024]{1,0:T(8,128)(2,1)} %shard_map.129.v0_ref), channel_id=1, source_target_pairs={{0,8},{4,12},{8,16},{12,20},{16,24},{20,28},{24,32},{28,36},{32,40... | collective-permute-start | bytes 786440 | tf_op jit(solution)/shard_map/ppermute | solution.py:371
  68.2 1.9 %collective-permute-start.6 = (bf16[128,1024]{1,0:T(8,128)(2,1)}, bf16[128,1024]{1,0:T(8,128)(2,1)S(1)}, u32[]{:S(2)}, u32[]{:S(2)}) collective-permute-start(bf16[128,1024]{1,0:T(8,128)(2,1)} %shard_map.129.v0_ref), channel_id=1, source_target_pairs={{0,4},{4,24},{8,12},{12,32},{16,20},{20,40},{24,28},{28,48},{32,36... | collective-permute-start | bytes 786440 | tf_op jit(solution)/shard_map/ppermute | solution.py:379
  70.1 1.9 %collective-permute-start.7 = (bf16[128,1024]{1,0:T(8,128)(2,1)}, bf16[128,1024]{1,0:T(8,128)(2,1)S(1)}, u32[]{:S(2)}, u32[]{:S(2)}) collective-permute-start(bf16[128,1024]{1,0:T(8,128)(2,1)} %shard_map.129.v0_ref), channel_id=1, source_target_pairs={{0,16},{4,20},{8,24},{12,28},{16,32},{20,36},{24,40},{28,44},{32,4... | collective-permute-start | bytes 786440 | tf_op jit(solution)/shard_map/ppermute | solution.py:371
  72.0 0.0 collective-permute-done.3.b_ref.k2_ref
  72.1 0.0 copy-start
  72.1 8.0 %collective-permute-start.4 = (bf16[2,128,1024]{2,1,0:T(8,128)(2,1)S(1)}, bf16[2,128,1024]{2,1,0:T(8,128)(2,1)S(1)}, u32[]{:S(2)}, u32[]{:S(2)}) collective-permute-start(bf16[2,128,1024]{2,1,0:T(8,128)(2,1)S(1)} %shard_map.131), channel_id=1, source_target_pairs={{0,4},{4,0},{8,12},{12,8},{16,20},{20,16},{24,28},{28,24},{32,36},... | collective-permute-start | bytes 1572872 | tf_op jit(solution)/shard_map/ppermute | solution.py:375
  80.1 8.3 %collective-permute-done.5.a_ref.v1_ref = bf16[128,1024]{1,0:T(8,128)(2,1)S(1)} collective-permute-done((bf16[128,1024]{1,0:T(8,128)(2,1)}, bf16[128,1024]{1,0:T(8,128)(2,1)S(1)}, u32[]{:S(2)}, u32[]{:S(2)}) %collective-permute-start.5) | collective-permute-done | bytes 262176 | tf_op jit(solution)/shard_map/ppermute | solution.py:371
  88.4 4.4 %collective-permute-done.6.v5_ref = bf16[128,1024]{1,0:T(8,128)(2,1)S(1)} collective-permute-done((bf16[128,1024]{1,0:T(8,128)(2,1)}, bf16[128,1024]{1,0:T(8,128)(2,1)S(1)}, u32[]{:S(2)}, u32[]{:S(2)}) %collective-permute-start.6) | collective-permute-done | bytes 262176 | tf_op jit(solution)/shard_map/ppermute | solution.py:379
  92.8 0.0 collective-permute-done.7.b_ref.v2_ref
  92.8 3.3 %collective-permute-start.8 = (bf16[2,128,1024]{2,1,0:T(8,128)(2,1)S(1)}, bf16[2,128,1024]{2,1,0:T(8,128)(2,1)S(1)}, u32[]{:S(2)}, u32[]{:S(2)}) collective-permute-start(bf16[2,128,1024]{2,1,0:T(8,128)(2,1)S(1)} %shard_map.133), channel_id=1, source_target_pairs={{0,4},{4,0},{8,12},{12,8},{16,20},{20,16},{24,28},{28,24},{32,36},... | collective-permute-start | bytes 1572872 | tf_op jit(solution)/shard_map/ppermute | solution.py:375
  96.1 0.0 collective-permute-done.4.swap_ref
  96.1 2.2 %shard_map.132 = (bf16[8,128,768]{2,1,0:T(8,128)(2,1)S(1)}, f32[128,128]{1,0:T(8,128)S(1)}) custom-call(s32[3]{0:T(128)S(1)} %pad_add_fusion.idx_ref, s32[1,6]{1,0:T(1,128)S(1)} %copy-done.4, bf16[128,1024]{1,0:T(8,128)(2,1)S(1)} %get-tuple-element.39.q_ref, bf16[128,1024]{1,0:T(8,128)(2,1)S(1)} %get-tuple-element.42.src_ref.k0_ref, ...), custom_call_target="tpu_custom_call" | custom-call | flops 1000000 | bytes 1000000 | tf_op jit(solution)/shard_map/pallas_call | solution.py:39
  98.3 0.0 collective-permute-done.8.swap_ref
  98.4 0.0 copy-start.3
  98.4 0.7 shard_map.134
  99.0 9.8 %psum.7.sq_ref = f32[1,128]{1,0:T(1,128)S(1)} all-reduce(f32[1,128]{1,0:T(1,128)S(1)} %get-tuple-element.49), channel_id=1, replica_groups=mesh['ctx'=128,'ch'=4] {'ch'}, use_global_device_ids=true, to_apply=%region_0.1 | all-reduce | flops 128 | bytes 1024 | tf_op jit(solution)/shard_map/psum | solution.py:480
  108.8 0.8 shard_map.135
  (18 shorter events, 0.2 us)
Async XLA Ops:
  0.6 4.7 %copy-start.7 = (f32[3,3,1024]{2,1,0:T(4,128)S(1)}, f32[3,3,1024]{2,1,0:T(4,128)}, u32[]{:S(2)}) copy-start(f32[3,3,1024]{2,1,0:T(4,128)} %param.14) | copy-start | bytes 110596
  0.6 4.7 %copy-start.5 = (f32[16,1024]{1,0:T(8,128)S(1)}, f32[16,1024]{1,0:T(8,128)}, u32[]{:S(2)}) copy-start(f32[16,1024]{1,0:T(8,128)} %param.15) | copy-start | bytes 196612
  0.7 4.7 %copy-start.6 = (f32[16,1024]{1,0:T(8,128)S(1)}, f32[16,1024]{1,0:T(8,128)}, u32[]{:S(2)}) copy-start(f32[16,1024]{1,0:T(8,128)} %param.16) | copy-start | bytes 196612
  2.2 5.1 %copy-start.8 = (s32[128]{0:T(128)S(1)}, s32[128]{0:T(128)}, u32[]{:S(2)}) copy-start(s32[128]{0:T(128)} %param.19) | copy-start | bytes 1540
  2.2 18.1 %collective-permute-start = (bf16[32,1024]{1,0:T(8,128)(2,1)}, bf16[32,1024]{1,0:T(8,128)(2,1)S(1)}, u32[]{:S(2)}, u32[]{:S(2)}) collective-permute-start(bf16[32,1024]{1,0:T(8,128)(2,1)} %shard_map.122), channel_id=1, source_target_pairs={{0,4},{4,8},{8,12},{12,16},{16,20},{20,24},{24,28},{28,32},{32,36}... | collective-permute-start | bytes 196616 | tf_op jit(solution)/shard_map/ppermute | solution.py:407
  5.3 20.2 %copy-start.1 = (bf16[128,1024]{1,0:T(8,128)(2,1)S(1)}, bf16[128,1024]{1,0:T(8,128)(2,1)}, u32[]{:S(2)}) copy-start(bf16[128,1024]{1,0:T(8,128)(2,1)} %q_hbm.3) | copy-start | bytes 786436
  5.3 20.2 %copy-start.2 = (bf16[128,1024]{1,0:T(8,128)(2,1)S(1)}, bf16[128,1024]{1,0:T(8,128)(2,1)}, u32[]{:S(2)}) copy-start(bf16[128,1024]{1,0:T(8,128)(2,1)} %k_hbm.3) | copy-start | bytes 786436
  21.0 17.0 %all-to-all-start = ((bf16[8,128,128]{2,1,0:T(8,128)(2,1)}), bf16[8,128,128]{2,1,0:T(8,128)(2,1)S(1)}, u32[]{:S(2)}, u32[]{:S(2)}) async-start(bf16[8,128,128]{2,1,0:T(8,128)(2,1)} %get-tuple-element.27), calls=%async_computation | async-start | bytes 524288 | tf_op jit(solution)/shard_map/all_to_all | solution.py:442
  25.9 30.7 %collective-permute-start.2 = (bf16[128,1024]{1,0:T(8,128)(2,1)S(1)}, bf16[128,1024]{1,0:T(8,128)(2,1)S(1)}, u32[]{:S(2)}, u32[]{:S(2)}) collective-permute-start(bf16[128,1024]{1,0:T(8,128)(2,1)S(1)} %get-tuple-element.42.src_ref.k0_ref), channel_id=1, source_target_pairs={{0,8},{4,12},{8,16},{12,20},{16,24},{20,28},{24,32},{28,36},{32,40... | collective-permute-start | bytes 786440 | tf_op jit(solution)/shard_map/ppermute | solution.py:371
  39.3 8.5 %all-to-all-start.1 = ((bf16[4,128,128]{2,1,0:T(8,128)(2,1)}), bf16[4,128,128]{2,1,0:T(8,128)(2,1)S(1)}, u32[]{:S(2)}, u32[]{:S(2)}) async-start(bf16[4,128,128]{2,1,0:T(8,128)(2,1)} %get-tuple-element.30), calls=%async_computation.1 | async-start | bytes 262144 | tf_op jit(solution)/shard_map/all_to_all | solution.py:449
  44.6 17.9 %collective-permute-start.1 = (bf16[128,1024]{1,0:T(8,128)(2,1)}, bf16[128,1024]{1,0:T(8,128)(2,1)S(1)}, u32[]{:S(2)}, u32[]{:S(2)}) collective-permute-start(bf16[128,1024]{1,0:T(8,128)(2,1)} %shard_map.128), channel_id=1, source_target_pairs={{0,4},{4,24},{8,12},{12,32},{16,20},{20,40},{24,28},{28,48},{32,36... | collective-permute-start | bytes 786440 | tf_op jit(solution)/shard_map/ppermute | solution.py:379
  49.1 13.9 %all-to-all-start.2 = ((bf16[4,128,128]{2,1,0:T(8,128)(2,1)}), bf16[4,128,128]{2,1,0:T(8,128)(2,1)S(1)}, u32[]{:S(2)}, u32[]{:S(2)}) async-start(bf16[4,128,128]{2,1,0:T(8,128)(2,1)} %shard_map.127), calls=%async_computation.2 | async-start | bytes 262144 | tf_op jit(solution)/shard_map/all_to_all | solution.py:455
  53.8 18.3 %collective-permute-start.3 = (bf16[128,1024]{1,0:T(8,128)(2,1)S(1)}, bf16[128,1024]{1,0:T(8,128)(2,1)S(1)}, u32[]{:S(2)}, u32[]{:S(2)}) collective-permute-start(bf16[128,1024]{1,0:T(8,128)(2,1)S(1)} %shard_map.130), channel_id=1, source_target_pairs={{0,16},{4,20},{8,24},{12,28},{16,32},{20,36},{24,40},{28,44},{32,4... | collective-permute-start | bytes 786440 | tf_op jit(solution)/shard_map/ppermute | solution.py:371
  63.0 33.1 %copy-start.4 = (s32[1,6]{1,0:T(1,128)S(1)}, s32[1,6]{1,0:T(1,128)}, u32[]{:S(2)}) copy-start(s32[1,6]{1,0:T(1,128)} %mask_ref.1) | copy-start | bytes 76
  65.0 23.4 %collective-permute-start.5 = (bf16[128,1024]{1,0:T(8,128)(2,1)}, bf16[128,1024]{1,0:T(8,128)(2,1)S(1)}, u32[]{:S(2)}, u32[]{:S(2)}) collective-permute-start(bf16[128,1024]{1,0:T(8,128)(2,1)} %shard_map.129.v0_ref), channel_id=1, source_target_pairs={{0,8},{4,12},{8,16},{12,20},{16,24},{20,28},{24,32},{28,36},{32,40... | collective-permute-start | bytes 786440 | tf_op jit(solution)/shard_map/ppermute | solution.py:371
  68.2 24.6 %collective-permute-start.6 = (bf16[128,1024]{1,0:T(8,128)(2,1)}, bf16[128,1024]{1,0:T(8,128)(2,1)S(1)}, u32[]{:S(2)}, u32[]{:S(2)}) collective-permute-start(bf16[128,1024]{1,0:T(8,128)(2,1)} %shard_map.129.v0_ref), channel_id=1, source_target_pairs={{0,4},{4,24},{8,12},{12,32},{16,20},{20,40},{24,28},{28,48},{32,36... | collective-permute-start | bytes 786440 | tf_op jit(solution)/shard_map/ppermute | solution.py:379
  70.1 22.7 %collective-permute-start.7 = (bf16[128,1024]{1,0:T(8,128)(2,1)}, bf16[128,1024]{1,0:T(8,128)(2,1)S(1)}, u32[]{:S(2)}, u32[]{:S(2)}) collective-permute-start(bf16[128,1024]{1,0:T(8,128)(2,1)} %shard_map.129.v0_ref), channel_id=1, source_target_pairs={{0,16},{4,20},{8,24},{12,28},{16,32},{20,36},{24,40},{28,44},{32,4... | collective-permute-start | bytes 786440 | tf_op jit(solution)/shard_map/ppermute | solution.py:371
  72.1 26.3 %copy-start = (bf16[128,1024]{1,0:T(8,128)(2,1)S(1)}, bf16[128,1024]{1,0:T(8,128)(2,1)}, u32[]{:S(2)}) copy-start(bf16[128,1024]{1,0:T(8,128)(2,1)} %shard_map.129.v0_ref) | copy-start | bytes 786436
  72.1 24.0 %collective-permute-start.4 = (bf16[2,128,1024]{2,1,0:T(8,128)(2,1)S(1)}, bf16[2,128,1024]{2,1,0:T(8,128)(2,1)S(1)}, u32[]{:S(2)}, u32[]{:S(2)}) collective-permute-start(bf16[2,128,1024]{2,1,0:T(8,128)(2,1)S(1)} %shard_map.131), channel_id=1, source_target_pairs={{0,4},{4,0},{8,12},{12,8},{16,20},{20,16},{24,28},{28,24},{32,36},... | collective-permute-start | bytes 1572872 | tf_op jit(solution)/shard_map/ppermute | solution.py:375
  92.8 5.5 %collective-permute-start.8 = (bf16[2,128,1024]{2,1,0:T(8,128)(2,1)S(1)}, bf16[2,128,1024]{2,1,0:T(8,128)(2,1)S(1)}, u32[]{:S(2)}, u32[]{:S(2)}) collective-permute-start(bf16[2,128,1024]{2,1,0:T(8,128)(2,1)S(1)} %shard_map.133), channel_id=1, source_target_pairs={{0,4},{4,0},{8,12},{12,8},{16,20},{20,16},{24,28},{28,24},{32,36},... | collective-permute-start | bytes 1572872 | tf_op jit(solution)/shard_map/ppermute | solution.py:375
  98.4 10.5 %copy-start.3 = (f32[1024]{0:T(1024)S(1)}, f32[1024]{0:T(1024)}, u32[]{:S(2)}) copy-start(f32[1024]{0:T(1024)} %param.21) | copy-start | bytes 12292
